TPU v7x, 256 devices: a whole 4x4x8 slice. The times are simulated.
256 devices in a mesh: ens: 16 (over y, x_hi, core), lat: 16 (over x_lo, z).
Axes of the slice: x: 4 (x_hi: 2, x_lo: 2; x = x_hi * 2 + x_lo), y: 4, z: 8, core: 2. Of those that a mesh axis runs over, the one named last changes fastest.
Arguments:
- grid: bfloat16 [16, 8, 512, 1440], P('ens', None, 'lat'), may hold values from -48 to 48
- legendre: bfloat16 [512, 384, 384], P('lat'), as said below
- target: float32 [384, 8, 2, 384], P('lat'), may hold values from -6 to 6
- owner: int32 [384], replicated, may hold values from 0 to 383, each once
- cutoff: int32 [8], replicated, may hold values from 90 to 360
Outputs:
- mean_score: float32 [1], replicated
- score_grad: bfloat16 [16, 8, 512, 1440], P('ens', None, 'lat')
Inputs may be any that keep to these rules, and one draw needn't show every extreme that they name: legendre is zero where l < m or l > 360. owner names each order 0 to 383 once; index j of lat owns slots j * 384 / 16 onward.
All inputs are finite; a program needn't handle non-finite values.
Results may differ from a plain program's by a relative error of at most 0.0075.
The roundings to bfloat16 on the way count: a program that leaves them out, or rounds other values in their place, can miss the bound.
Values may be sent and summed in bfloat16 or wider, within the bound.
No kernel may reach another device: no remote copies, remote signals or barrier semaphores. Data moves between devices by JAX's collectives and lax.ppermute only.
A program may use at most 128 MiB of HBM per device.

v0:
```python
import math

import jax
import jax.numpy as jnp
import numpy as np
from jax import lax
from jax.experimental import pallas as pl
from jax.experimental.pallas import tpu as pltpu
from jax.sharding import PartitionSpec as P

delta_abs = 0.1
both_axes = ("lat", "ens")


def wave_table(mode_count, lon_count):
    points = np.arange(lon_count, dtype=np.int64)
    modes = np.arange(mode_count, dtype=np.int64)
    phase = modes[:, None] * points[None, :] % lon_count
    angle = phase.astype(np.float32) * np.float32(2.0 * math.pi / lon_count)
    both = np.stack([np.cos(angle), -np.sin(angle)]) / np.float32(math.sqrt(lon_count))
    return both.astype(np.float32).astype(jnp.bfloat16)


def column_of(codes_ref, row):
    line = codes_ref[row:row + 1, :]
    return jnp.transpose(jnp.broadcast_to(line, (128, 512)), (1, 0))

def pick_rows(codes_ref, row):
    column = column_of(codes_ref, row)
    lane = lax.broadcasted_iota(jnp.int32, (512, 128), 1).astype(jnp.float32)
    return jnp.concatenate(
        [jnp.where(column == lane + 128.0 * t, 1.0, 0.0).astype(jnp.bfloat16) for t in range(6)], axis=1)

def send_kernel(codes_ref, grid_ref, waves_ref, bands_ref, out_ref, four_ref):
    four_ref[...] = lax.dot_general(waves_ref[...], grid_ref[...], (((1,), (1,)), ((), ())),
        preferred_element_type=jnp.float32).astype(jnp.bfloat16)
    full = pick_rows(codes_ref, 0)
    half = pick_rows(codes_ref, 1)
    side = pick_rows(codes_ref, 2)
    dot = lambda a, b: jnp.dot(a, b, preferred_element_type=jnp.float32)
    out_ref[:, 0:256] = dot(full, four_ref[...]).astype(jnp.bfloat16)
    out_ref[:, 384:768] = dot(full, bands_ref[...]).astype(jnp.bfloat16)
    out_ref[:, 768:1152] = dot(half, bands_ref[...]).astype(jnp.bfloat16)
    both = dot(side, four_ref[...])
    odd = lax.broadcasted_iota(jnp.int32, (512, 128), 0) % 2
    out_ref[:, 256:384] = jnp.where(odd == 0, both[:, :128], both[:, 128:]).astype(jnp.bfloat16)

def send_call(codes, grid, waves, bands):
    vm = pl.BlockSpec(memory_space=pltpu.VMEM)
    return pl.pallas_call(send_kernel, out_shape=jax.ShapeDtypeStruct((512, 1152), jnp.bfloat16),
        in_specs=[vm]*4, out_specs=vm, scratch_shapes=[pltpu.VMEM((768, 256), jnp.bfloat16)],
        compiler_params=pltpu.CompilerParams(vmem_limit_bytes=40*1024*1024))(codes, grid, waves, bands)

def home_kernel(codes_ref, got_ref, waves_ref, out_ref):
    row = lax.broadcasted_iota(jnp.int32, (768, 512), 0).astype(jnp.float32)
    full = jnp.where(row == codes_ref[0:1, :], 1.0, 0.0).astype(jnp.bfloat16)
    side = jnp.where(row == codes_ref[2:3, :], 1.0, 0.0).astype(jnp.bfloat16)
    odd = lax.broadcasted_iota(jnp.int32, (512, 128), 0) % 2
    third = got_ref[:, 256:384]
    zero = jnp.zeros_like(third)
    wide = jnp.concatenate([jnp.where(odd == 0, third, zero), jnp.where(odd == 1, third, zero)], axis=1)
    natural = (jnp.dot(full, got_ref[:, 0:256], preferred_element_type=jnp.float32)
        + jnp.dot(side, wide, preferred_element_type=jnp.float32)).astype(jnp.bfloat16)
    out_ref[...] = lax.dot_general(natural, waves_ref[...], (((0,), (0,)), ((), ())),
        preferred_element_type=jnp.float32).astype(jnp.bfloat16)

def home_call(codes, got, waves):
    vm = pl.BlockSpec(memory_space=pltpu.VMEM)
    return pl.pallas_call(home_kernel, out_shape=jax.ShapeDtypeStruct((256, 1440), jnp.bfloat16),
        in_specs=[vm]*3, out_specs=vm,
        compiler_params=pltpu.CompilerParams(vmem_limit_bytes=40*1024*1024))(codes, got, waves)

def score_kernel(orders_ref, got_ref, target_ref, cutoff_ref, back_ref,
                 rows_ref, tiled_ref, coeffs_ref, grads_ref, wide_ref):
    lane_field = lax.broadcasted_iota(jnp.int32, (32, 128), 1) // 32
    for j in range(16):
        for q in range(3):
            block = got_ref[32 * j:32 * j + 32, 128 * q:128 * q + 128]
            for k in range(4):
                row = (q * 4 + k) * 32
                rows_ref[row:row + 32, 128 * j:128 * j + 128] = jnp.where(
                    lane_field == k, block, jnp.zeros_like(block))
        band = got_ref[32 * j:32 * j + 32, 384:1152]
        for k in range(4):
            tiled_ref[128 * j + 32 * k:128 * j + 32 * k + 32, :] = band
    full = jnp.dot(rows_ref[0:256, :], tiled_ref[:, 0:384], preferred_element_type=jnp.float32)
    half = jnp.dot(rows_ref[256:384, :], tiled_ref[:, 384:768], preferred_element_type=jnp.float32)
    for third in range(3):
        coeffs_ref[third, 0:256, :] = full[:, 128 * third:128 * third + 128]
        coeffs_ref[third, 256:384, :] = half[:, 128 * third:128 * third + 128]
    offset = delta_abs * delta_abs
    limit = cutoff_ref[...]

    def column(third, part, order, load, store):
        lanes = pl.ds(pl.multiple_of(third * 128, 128), 128)
        level = lax.broadcasted_iota(jnp.int32, (8, 128), 1) + third * 128
        inside = (level >= order) & (level <= limit)
        goal = target_ref[pl.ds(pl.multiple_of(part * 8, 8), 8), lanes]
        member = [load(e) for e in range(16)]
        slope = [jnp.zeros((8, 128), jnp.float32) for _ in range(16)]
        pair_value = jnp.zeros((8, 128), jnp.float32)
        for i in range(16):
            for k in range(i + 1, 16):
                spread = member[i] - member[k]
                square = spread * spread + offset
                inverse = lax.rsqrt(square)
                step_slope = spread * inverse
                slope[i] = slope[i] + step_slope
                slope[k] = slope[k] - step_slope
                pair_value = pair_value + (square * inverse - delta_abs)
        own_value = jnp.zeros((8, 128), jnp.float32)
        for i in range(16):
            spread = member[i] - goal
            square = spread * spread + offset
            inverse = lax.rsqrt(square)
            own_value = own_value + (square * inverse - delta_abs)
            grad = spread * inverse - slope[i] / 16.0
            store(i, jnp.where(inside, grad, 0.0))
        return jnp.where(inside, own_value / 16.0 - pair_value / 256.0, 0.0)

    def full_column(step, total):
        part = step // 3
        third = step % 3
        def load(e):
            return coeffs_ref[third, pl.ds(2 * e + part, 8, stride=32), :]
        def store(e, value):
            grads_ref[third, pl.ds(2 * e + part, 8, stride=32), :] = value
        return total + column(third, part, orders_ref[0], load, store)

    def half_column(third, total):
        def load(e):
            return jnp.concatenate([coeffs_ref[third, pl.ds(256 + 2 * e + h, 4, stride=32), :] for h in range(2)])
        def store(e, value):
            for h in range(2):
                grads_ref[third, pl.ds(256 + 2 * e + h, 4, stride=32), :] = value[4 * h:4 * h + 4]
        return total + column(third, 2, orders_ref[1], load, store)

    total = lax.fori_loop(0, 6, full_column, jnp.zeros((8, 128), jnp.float32))
    total = lax.fori_loop(0, 3, half_column, total)
    score = jnp.sum(jnp.sum(total, axis=1, keepdims=True), axis=0, keepdims=True)
    high = score.astype(jnp.bfloat16).astype(jnp.float32)
    middle = (score - high).astype(jnp.bfloat16).astype(jnp.float32)
    low = score - high - middle
    spot = lax.broadcasted_iota(jnp.int32, (512, 128), 1)
    pieces = jnp.where(spot == 0, high, jnp.where(spot == 1, middle, jnp.where(spot == 2, low, 0.0)))
    back_ref[:, 384:512] = pieces.astype(jnp.bfloat16)

    grads = jnp.concatenate([grads_ref[third] for third in range(3)], axis=1).astype(jnp.bfloat16)
    dims = (((1,), (1,)), ((), ()))
    wide_ref[0:256, :] = lax.dot_general(grads[0:256], tiled_ref[:, 0:384], dims, preferred_element_type=jnp.float32)
    wide_ref[256:384, :] = lax.dot_general(grads[256:384], tiled_ref[:, 384:768], dims, preferred_element_type=jnp.float32)
    for j in range(16):
        for q in range(3):
            merged = wide_ref[q * 128:q * 128 + 32, 128 * j:128 * j + 128]
            for k in range(1, 4):
                row = (q * 4 + k) * 32
                merged = jnp.where(lane_field == k, wide_ref[row:row + 32, 128 * j:128 * j + 128], merged)
            back_ref[32 * j:32 * j + 32, 128 * q:128 * q + 128] = merged.astype(jnp.bfloat16)

def score_call(orders, got, target_rows, limit):
    vm = pl.BlockSpec(memory_space=pltpu.VMEM)
    return pl.pallas_call(score_kernel, out_shape=jax.ShapeDtypeStruct((512, 512), jnp.bfloat16),
        in_specs=[pl.BlockSpec(memory_space=pltpu.SMEM), vm, vm, vm], out_specs=vm,
        scratch_shapes=[pltpu.VMEM((384, 2048), jnp.bfloat16), pltpu.VMEM((2048, 768), jnp.bfloat16),
            pltpu.VMEM((3, 384, 128), jnp.float32), pltpu.VMEM((3, 384, 128), jnp.float32),
            pltpu.VMEM((384, 2048), jnp.float32)],
        compiler_params=pltpu.CompilerParams(vmem_limit_bytes=40*1024*1024))(orders, got, target_rows, limit)


def body(grid, legendre, target, owner, cutoff):
    fields, rows, lon_count = grid.shape[1:]
    modes = legendre.shape[1]
    e = lax.axis_index("ens")
    j = lax.axis_index("lat")
    waves = jnp.asarray(wave_table(modes, lon_count).reshape(2 * modes, lon_count))
    by_lat = owner.reshape(16, 24)
    order_full = jnp.repeat(by_lat[:, :16].reshape(256), 2)
    order_half = jnp.repeat(by_lat[:, 16:].reshape(128), 4)
    place = jnp.arange(512, dtype=jnp.int32)
    codes = jnp.stack([
        order_full + modes * (place % 2),
        order_half + modes * (place % 2),
        order_half + modes * (place // 2 % 2),
    ]).astype(jnp.float32)
    codes = jnp.concatenate([codes, jnp.zeros((5, 512), jnp.float32)])
    bands = lax.dynamic_slice_in_dim(legendre, 2 * e, 2, axis=0).reshape(2 * modes, -1)
    sent = send_call(codes, grid.reshape(fields * rows, lon_count), waves, bands)
    got = lax.all_to_all(
        sent.reshape(256, 2, 1152), both_axes, split_axis=0, concat_axis=0, tiled=True
    ).reshape(512, 1152)

    full_slot = e
    half_slot = 16 + e // 2
    side = e % 2
    own_orders = lax.dynamic_slice_in_dim(owner, 24 * j, 24)
    orders = jnp.stack([own_orders[full_slot], own_orders[half_slot]])
    full_rows = lax.dynamic_index_in_dim(target, full_slot, 0, keepdims=False)
    half_rows = lax.dynamic_slice(target, (half_slot, 0, side, 0), (1, fields, 1, target.shape[3]))
    target_rows = jnp.concatenate([full_rows[:, 0], full_rows[:, 1], half_rows[0, :, 0]])
    limit = jnp.broadcast_to(cutoff[:, None], (fields, 128))
    back = score_call(orders, got, target_rows, limit)
    home = lax.all_to_all(
        back.reshape(256, 2, 512), both_axes, split_axis=0, concat_axis=0, tiled=True
    ).reshape(512, 512)
    score_sum = jnp.sum(home[::2, 384:387].astype(jnp.float32))
    cut_level = cutoff.astype(jnp.float32)
    modes_valid = jnp.sum((cut_level + 1.0) * (cut_level + 2.0))
    mean_score = (score_sum / modes_valid).reshape(1)
    grid_grad = home_call(codes, home, waves)
    return (mean_score, grid_grad.reshape(1, fields, rows, lon_count))


def solution(mesh):
    in_specs = (
        P("ens", None, "lat", None),
        P("lat", None, None),
        P("lat", None, None, None),
        P(),
        P(),
    )
    out_specs = (P(), P("ens", None, "lat", None))
    return jax.shard_map(body, mesh=mesh, in_specs=in_specs, out_specs=out_specs, check_vma=False)
```

profile of v0, /device:TPU:1, one launch (start us, length us, event | category | flops | bytes accessed | tf_op | source)
XLA Modules:
  0.0 100.6 jit_solution(4792570401169732783)
XLA Ops:
  0.6 0.0 copy-start
  0.6 0.0 copy-start.3
  0.7 0.9 reshape.164
  1.5 0.1 slice.21
  1.6 0.1 reshape.167
  1.7 0.1 broadcast_in_dim.14
  1.8 0.1 reshape.168
  1.9 0.1 reshape.165
  2.0 0.1 broadcast_in_dim.6
  2.1 0.1 reshape.166
  2.3 1.1 %constant_dynamic-slice_fusion.2 = bf16[2,384,384]{2,1,0:T(8,128)(2,1)S(1)} fusion(bf16[32,384,384]{2,1,0:T(8,128)(2,1)} %param.7, s32[]{:T(128)S(6)} %select_n.89), kind=kLoop, calls=%fused_computation.23 | loop fusion | bytes 1179652 | tf_op jit(solution)/shard_map/dynamic_slice | solution.py:186
  3.4 0.0 copy-done.3
  3.4 0.0 copy-start.1
  3.5 1.7 %copy-done.1 = bf16[768,1440]{1,0:T(8,128)(2,1)S(1)} copy-done((bf16[768,1440]{1,0:T(8,128)(2,1)S(1)}, bf16[768,1440]{1,0:T(8,128)(2,1)}, u32[]{:S(2)}) %copy-start.1) | copy-done | bytes 2211864
  5.1 3.3 %shard_map.77 = bf16[512,1152]{1,0:T(8,128)(2,1)S(1)} custom-call(f32[8,512]{1,0:T(8,128)S(1)} %concatenate.6.codes_ref, bf16[256,1440]{1,0:T(8,128)(2,1)S(1)} %bitcast.16, bf16[768,1440]{1,0:T(8,128)(2,1)S(1)} %copy-done.1, bf16[768,384]{1,0:T(8,128)(2,1)S(1)} %bitcast.15), custom_call_target="tpu_custom_call" | custom-call | tf_op jit(solution)/shard_map/pallas_call | solution.py:50
  8.4 1.3 %reshape.171 = bf16[256,2,1152]{2,1,0:T(2,128)(2,1)} reshape(bf16[512,1152]{1,0:T(8,128)(2,1)S(1)} %shard_map.77) | data formatting | bytes 2359296 | tf_op jit(solution)/shard_map/reshape | solution.py:189
  9.7 0.0 copy-start.4
  9.7 15.7 %all-to-all-start = ((bf16[256,2,1152]{2,1,0:T(2,128)(2,1)}), bf16[256,2,1152]{2,1,0:T(2,128)(2,1)S(1)}, u32[]{:S(2)}, u32[]{:S(2)}) async-start(bf16[256,2,1152]{2,1,0:T(2,128)(2,1)} %reshape.171), calls=%async_computation | async-start | bytes 2359296 | tf_op jit(solution)/shard_map/all_to_all | solution.py:188
  25.4 0.0 copy-done
  25.5 0.0 copy-done.4
  25.5 0.6 fusion.6
  26.1 1.4 %pad_add_fusion.orders_ref = s32[2]{0:T(128)S(1)} fusion(s32[1]{0:T(128)} %get-tuple-element.7, s32[1]{0:T(128)} %get-tuple-element.6), kind=kLoop, calls=%fused_computation.24 | loop fusion | flops 2 | bytes 16 | tf_op jit(solution)/shard_map/stack | solution.py:196
  27.5 0.0 copy-start.5
  27.5 31.4 %all-to-all-done = bf16[256,2,1152]{2,1,0:T(2,128)(2,1)S(1)} async-done(((bf16[256,2,1152]{2,1,0:T(2,128)(2,1)}), bf16[256,2,1152]{2,1,0:T(2,128)(2,1)S(1)}, u32[]{:S(2)}, u32[]{:S(2)}) %all-to-all-start) | async-done | bytes 1179680 | tf_op jit(solution)/shard_map/all_to_all | solution.py:188
  58.9 0.5 reshape.172.got_ref
  59.4 0.0 copy-done.5
  59.4 0.1 broadcast_in_dim.15.cutoff_ref
  59.4 5.0 %shard_map.78 = bf16[512,512]{1,0:T(8,128)(2,1)S(1)} custom-call(s32[2]{0:T(128)S(1)} %pad_add_fusion.orders_ref, bf16[512,1152]{1,0:T(8,128)(2,1)S(1)} %reshape.172.got_ref, f32[24,384]{1,0:T(8,128)S(1)} %pad_maximum_fusion.target_ref, s32[8,128]{1,0:T(8,128)S(1)} %broadcast_in_dim.15.cutoff_ref), custom_call_target="tpu_custom_call" | custom-call | tf_op jit(solution)/shard_map/pallas_call | solution.py:162
  64.5 0.0 copy-start.2
  64.5 1.0 reshape.173
  65.5 7.9 %all-to-all-start.1 = ((bf16[256,2,512]{2,1,0:T(2,128)(2,1)}), bf16[256,2,512]{2,1,0:T(2,128)(2,1)}, u32[]{:S(2)}, u32[]{:S(2)}) async-start(bf16[256,2,512]{2,1,0:T(2,128)(2,1)} %reshape.173), calls=%async_computation.1 | async-start | bytes 1048576 | tf_op jit(solution)/shard_map/all_to_all | solution.py:202
  73.3 0.6 multiply_reduce_fusion
  74.0 19.3 %all-to-all-done.1 = bf16[256,2,512]{2,1,0:T(2,128)(2,1)} async-done(((bf16[256,2,512]{2,1,0:T(2,128)(2,1)}), bf16[256,2,512]{2,1,0:T(2,128)(2,1)}, u32[]{:S(2)}, u32[]{:S(2)}) %all-to-all-start.1) | async-done | bytes 524320 | tf_op jit(solution)/shard_map/all_to_all | solution.py:202
  93.3 1.2 %reshape.174.got_ref = bf16[512,512]{1,0:T(8,128)(2,1)S(1)} reshape(bf16[256,2,512]{2,1,0:T(2,128)(2,1)} %all-to-all-done.1) | data formatting | bytes 1048576 | tf_op jit(solution)/shard_map/reshape | solution.py:204
  94.5 0.1 slice.19
  94.7 0.0 copy-done.2
  94.7 2.9 %shard_map.79 = bf16[256,1440]{1,0:T(8,128)(2,1)} custom-call(f32[8,512]{1,0:T(8,128)S(1)} %concatenate.6.codes_ref, bf16[512,512]{1,0:T(8,128)(2,1)S(1)} %reshape.174.got_ref, bf16[768,1440]{1,0:T(8,128)(2,1)S(1)} %copy-done.2), custom_call_target="tpu_custom_call" | custom-call | tf_op jit(solution)/shard_map/pallas_call | solution.py:69
  97.6 0.6 convert_reduce_fusion
  (9 shorter events, 0.1 us)
Async XLA Ops:
  0.6 24.8 %copy-start = (f32[24,8,2,384]{3,2,1,0:T(2,128)S(1)}, f32[24,8,2,384]{3,2,1,0:T(2,128)}, u32[]{:S(2)}) copy-start(f32[24,8,2,384]{3,2,1,0:T(2,128)} %param.8) | copy-start | bytes 1769476
  0.6 2.8 %copy-start.3 = (bf16[1,8,32,1440]{3,2,1,0:T(8,128)(2,1)S(1)}, bf16[1,8,32,1440]{3,2,1,0:T(8,128)(2,1)}, u32[]{:S(2)}) copy-start(bf16[1,8,32,1440]{3,2,1,0:T(8,128)(2,1)} %param.6) | copy-start | bytes 2211844
  3.4 1.7 %copy-start.1 = (bf16[768,1440]{1,0:T(8,128)(2,1)S(1)}, bf16[768,1440]{1,0:T(8,128)(2,1)}, u32[]{:S(2)}) copy-start(bf16[768,1440]{1,0:T(8,128)(2,1)} %constant.94.clone.waves_ref) | copy-start | bytes 6635524
  9.7 15.8 %copy-start.4 = (s32[384]{0:T(512)S(1)}, s32[384]{0:T(512)}, u32[]{:S(2)}) copy-start(s32[384]{0:T(512)} %param.9) | copy-start | bytes 4612
  9.7 49.2 %all-to-all-start = ((bf16[256,2,1152]{2,1,0:T(2,128)(2,1)}), bf16[256,2,1152]{2,1,0:T(2,128)(2,1)S(1)}, u32[]{:S(2)}, u32[]{:S(2)}) async-start(bf16[256,2,1152]{2,1,0:T(2,128)(2,1)} %reshape.171), calls=%async_computation | async-start | bytes 2359296 | tf_op jit(solution)/shard_map/all_to_all | solution.py:188
  27.5 31.9 %copy-start.5 = (s32[8]{0:T(128)S(1)}, s32[8]{0:T(128)}, u32[]{:S(2)}) copy-start(s32[8]{0:T(128)} %param.10) | copy-start | bytes 100
  64.5 30.2 %copy-start.2 = (bf16[768,1440]{1,0:T(8,128)(2,1)S(1)}, bf16[768,1440]{1,0:T(8,128)(2,1)}, u32[]{:S(2)}) copy-start(bf16[768,1440]{1,0:T(8,128)(2,1)} %constant.94.clone.waves_ref) | copy-start | bytes 6635524
  65.5 27.8 %all-to-all-start.1 = ((bf16[256,2,512]{2,1,0:T(2,128)(2,1)}), bf16[256,2,512]{2,1,0:T(2,128)(2,1)}, u32[]{:S(2)}, u32[]{:S(2)}) async-start(bf16[256,2,512]{2,1,0:T(2,128)(2,1)} %reshape.173), calls=%async_computation.1 | async-start | bytes 1048576 | tf_op jit(solution)/shard_map/all_to_all | solution.py:202
where the time goes:
time: 101 us
  waiting for transfers between devices  50.7 us (50%)
  starting transfers between devices  23.5 us (23%)
  Pallas kernels  11.3 us (11%)
  local copies, waits for them, and re-layouts  9.21 us (9%)
  between operations  3.32 us (3%)
  other arithmetic  2.65 us (3%)
    all_to_all x1, waiting for transfers between devices, body(): lax.all_to_all(sent.reshape(256, 2, 1152), both_axes, split_axis=0, conca...  31.4 us
    all_to_all x1, waiting for transfers between devices, body(): lax.all_to_all(back.reshape(256, 2, 512), both_axes, split_axis=0, concat...  19.3 us
    all_to_all x1, starting transfers between devices, body(): lax.all_to_all(sent.reshape(256, 2, 1152), both_axes, split_axis=0, conca...  15.7 us
    all_to_all x1, starting transfers between devices, body(): lax.all_to_all(back.reshape(256, 2, 512), both_axes, split_axis=0, concat...  7.86 us
    pallas_call x1, Pallas kernels, score_call(): pl.pallas_call(score_kernel, out_shape=jax.ShapeDtypeStruct((512, 512), j...  5.03 us
    pallas_call x1, Pallas kernels, send_call(): pl.pallas_call(send_kernel, out_shape=jax.ShapeDtypeStruct((512, 1152), j...  3.32 us
    pallas_call x1, Pallas kernels, home_call(): pl.pallas_call(home_kernel, out_shape=jax.ShapeDtypeStruct((256, 1440), j...  2.91 us
  transfers between devices with their start and end apart: 2, of which 2 were waited for; matrix products, arithmetic and copies ran while one was open for 3% of the time, Pallas kernels for 0%

commit v1 on v0

v1 whole, which is shorter than its diff:
```python
import math

import jax
import jax.numpy as jnp
import numpy as np
from jax import lax
from jax.experimental import pallas as pl
from jax.experimental.pallas import tpu as pltpu
from jax.sharding import PartitionSpec as P

delta_abs = 0.1
both_axes = ("lat", "ens")


def wave_table(mode_count, lon_count):
    points = np.arange(lon_count, dtype=np.int64)
    modes = np.arange(mode_count, dtype=np.int64)
    phase = modes[:, None] * points[None, :] % lon_count
    angle = phase.astype(np.float32) * np.float32(2.0 * math.pi / lon_count)
    both = np.stack([np.cos(angle), -np.sin(angle)]) / np.float32(math.sqrt(lon_count))
    return both.astype(np.float32).astype(jnp.bfloat16)


def dot(left, right):
    return jnp.dot(left, right, preferred_element_type=jnp.float32)


def flag(condition):
    return jnp.where(condition, 1.0, 0.0).astype(jnp.bfloat16)


def iota(shape, axis):
    return lax.broadcasted_iota(jnp.int32, shape, axis)


def send_kernel(
    place_ref, owner_ref, grid_hbm, waves_hbm, legendre_hbm, out_ref, codes_ref,
    grid_ref, waves_ref, bands_ref, table_ref, four_ref, mix_ref, sems,
):
    grid_copy = pltpu.make_async_copy(grid_hbm, grid_ref, sems.at[0])
    band_copy = pltpu.make_async_copy(
        legendre_hbm.at[pl.ds(2 * place_ref[0], 2)], bands_ref, sems.at[1]
    )
    wave_copies = [
        pltpu.make_async_copy(
            waves_hbm.at[pl.ds(384 * c, 384)], waves_ref.at[pl.ds(384 * c, 384)], sems.at[2 + c]
        )
        for c in range(2)
    ]
    band_copy.start()
    grid_copy.start()
    for copy in wave_copies:
        copy.start()

    line = jnp.broadcast_to(owner_ref[...].astype(jnp.float32), (128, 384))
    column = jnp.transpose(line, (1, 0))
    lane = iota((384, 128), 1).astype(jnp.float32)
    held = jnp.concatenate([flag(column == lane + 128.0 * t) for t in range(3)], axis=1)
    group = flag(iota((16, 384), 1) // 24 == iota((16, 384), 0))
    lat_of = dot(group, held)
    before = flag(iota((384, 384), 0) < iota((384, 384), 1))
    count = dot(lat_of.astype(jnp.bfloat16), before)
    rank = jnp.sum(lat_of * count, axis=0, keepdims=True)
    lat = jnp.sum(lat_of * iota((16, 384), 0).astype(jnp.float32), axis=0, keepdims=True)
    full_code = jnp.where(rank < 16.0, lat * 16.0 + rank, -1.0)
    half_code = jnp.where(rank >= 16.0, lat * 8.0 + (23.0 - rank), -1.0)
    codes_ref[0:1, :] = full_code
    codes_ref[1:2, :] = half_code
    codes_ref[2:8, :] = jnp.zeros((6, 384), jnp.float32)
    full, even, odd, half = picks(full_code, half_code)

    both = jnp.concatenate([full, half], axis=1)
    band_copy.wait()
    for r in range(2):
        rows = bands_ref[r]
        table_ref[0:384, 0:384] = rows
        table_ref[0:384, 384:512] = jnp.zeros((384, 128), jnp.bfloat16)
        wide = jnp.concatenate([rows.astype(jnp.float32), jnp.zeros((384, 128), jnp.float32)], axis=1)
        for shift in range(1, 13):
            low = max(368 - 32 * shift, 0)
            high = 400 - 32 * shift
            if shift == 1:
                high = 384
                table_ref[384 + 368:768, :] = wide[368:384].astype(jnp.bfloat16)
                high = 368
            moved = pltpu.roll(wide[low:high], 32 * shift, 1)
            table_ref[384 + low:384 + high, :] = moved.astype(jnp.bfloat16)
        packed = dot(both, table_ref[...])
        for t in range(4):
            mix_ref[3 + t, pl.ds(r, 256, stride=2), :] = packed[:, 128 * t:128 * t + 128]

    grid_copy.wait()
    for c in range(2):
        wave_copies[c].wait()
        four_ref[384 * c:384 * c + 384, :] = lax.dot_general(
            waves_ref[384 * c:384 * c + 384, :], grid_ref[...], (((1,), (1,)), ((), ())),
            preferred_element_type=jnp.float32,
        ).astype(jnp.bfloat16)
        part = dot(full, four_ref[384 * c:384 * c + 384, :])
        for h in range(2):
            mix_ref[h, pl.ds(c, 256, stride=2), :] = part[:, 128 * h:128 * h + 128]
    part = dot(jnp.concatenate([even, odd], axis=1), four_ref[...])
    for h in range(2):
        mix_ref[2, pl.ds(h, 256, stride=2), :] = part[:, 128 * h:128 * h + 128]
    for t in range(7):
        out_ref[:, 128 * t:128 * t + 128] = mix_ref[t].astype(jnp.bfloat16)


def picks(full_code, half_code):
    row = iota((256, 384), 0)
    full = flag(row.astype(jnp.float32) == full_code)
    match = (row // 2).astype(jnp.float32) == half_code
    even = flag(match & (row % 2 == 0))
    odd = flag(match & (row % 2 == 1))
    return full, even, odd, flag(match)


def send_call(place, owner, grid, waves, legendre):
    vmem = pl.BlockSpec(memory_space=pltpu.VMEM)
    anywhere = pl.BlockSpec(memory_space=pltpu.HBM)
    return pl.pallas_call(
        send_kernel,
        out_shape=(
            jax.ShapeDtypeStruct((512, 896), jnp.bfloat16),
            jax.ShapeDtypeStruct((8, 384), jnp.float32),
        ),
        in_specs=[pl.BlockSpec(memory_space=pltpu.SMEM), vmem, anywhere, anywhere, anywhere],
        out_specs=(vmem, vmem),
        scratch_shapes=[
            pltpu.VMEM((256, 1440), jnp.bfloat16),
            pltpu.VMEM((768, 1440), jnp.bfloat16),
            pltpu.VMEM((2, 384, 384), jnp.bfloat16),
            pltpu.VMEM((768, 512), jnp.bfloat16),
            pltpu.VMEM((768, 256), jnp.bfloat16),
            pltpu.VMEM((7, 512, 128), jnp.float32),
            pltpu.SemaphoreType.DMA((4,)),
        ],
        compiler_params=pltpu.CompilerParams(vmem_limit_bytes=20 * 1024 * 1024),
    )(place, owner, grid, waves, legendre)


def score_kernel(
    orders_ref, got_ref, full_ref, half_ref, cutoff_ref, back_ref,
    rows_ref, tiled_ref, coeffs_ref, grads_ref, wide_ref,
):
    lane_field = iota((32, 128), 1) // 32
    for j in range(16):
        for q in range(3):
            block = got_ref[32 * j:32 * j + 32, 128 * q:128 * q + 128]
            for k in range(4):
                row = (q * 4 + k) * 32
                rows_ref[row:row + 32, 128 * j:128 * j + 128] = jnp.where(
                    lane_field == k, block, jnp.zeros_like(block)
                )
        band = got_ref[32 * j:32 * j + 32, 384:896]
        for k in range(4):
            tiled_ref[128 * j + 32 * k:128 * j + 32 * k + 32, :] = band
    coeffs = dot(rows_ref[...], tiled_ref[...])
    for t in range(4):
        coeffs_ref[t] = coeffs[:, 128 * t:128 * t + 128]
    offset = delta_abs * delta_abs
    limit = cutoff_ref[...]

    def column(level, order, goal, load, store):
        inside = (level >= order) & (level <= limit)
        member = [load(e) for e in range(16)]
        slope = [jnp.zeros((8, 128), jnp.float32) for _ in range(16)]
        pair_value = jnp.zeros((8, 128), jnp.float32)
        for i in range(16):
            for k in range(i + 1, 16):
                spread = member[i] - member[k]
                square = spread * spread + offset
                inverse = lax.rsqrt(square)
                step_slope = spread * inverse
                slope[i] = slope[i] + step_slope
                slope[k] = slope[k] - step_slope
                pair_value = pair_value + (square * inverse - delta_abs)
        own_value = jnp.zeros((8, 128), jnp.float32)
        for i in range(16):
            spread = member[i] - goal
            square = spread * spread + offset
            inverse = lax.rsqrt(square)
            own_value = own_value + (square * inverse - delta_abs)
            store(i, jnp.where(inside, spread * inverse - slope[i] / 16.0, 0.0))
        return jnp.where(inside, own_value / 16.0 - pair_value / 256.0, 0.0)

    def full_column(step, total):
        part = step // 3
        third = step % 3
        lanes = pl.ds(pl.multiple_of(third * 128, 128), 128)

        def load(e):
            return coeffs_ref[third, pl.ds(2 * e + part, 8, stride=32), :]

        def store(e, value):
            grads_ref[pl.ds(pl.multiple_of(part * 128 + 8 * e, 8), 8), lanes] = value

        goal = full_ref[pl.ds(pl.multiple_of(part * 8, 8), 8), lanes]
        return total + column(iota((8, 128), 1) + third * 128, orders_ref[0], goal, load, store)

    def half_column(tile, total):
        lanes = pl.ds(pl.multiple_of(tile * 128, 128), 128)

        def load(e):
            return jnp.concatenate(
                [coeffs_ref[tile, pl.ds(256 + 2 * e + h, 4, stride=32), :] for h in range(2)]
            )

        def store(e, value):
            grads_ref[256 + 8 * e:256 + 8 * e + 8, lanes] = value

        level = iota((8, 128), 1) + tile * 128 - orders_ref[2]
        level = jnp.where(level < 0, level + 512, level)
        return total + column(level, orders_ref[1], half_ref[:, lanes], load, store)

    total = lax.fori_loop(0, 6, full_column, jnp.zeros((8, 128), jnp.float32))
    total = lax.fori_loop(0, 4, half_column, total)
    grads_ref[0:256, 384:512] = jnp.zeros((256, 128), jnp.float32)
    score = jnp.sum(jnp.sum(total, axis=1, keepdims=True), axis=0, keepdims=True)
    high = score.astype(jnp.bfloat16).astype(jnp.float32)
    middle = (score - high).astype(jnp.bfloat16).astype(jnp.float32)
    low = score - high - middle
    spot = iota((128, 128), 1)
    pieces = jnp.where(spot == 96, high, jnp.where(spot == 97, middle, jnp.where(spot == 98, low, 0.0)))

    wide_ref[...] = lax.dot_general(
        grads_ref[...].astype(jnp.bfloat16), tiled_ref[...], (((1,), (1,)), ((), ())),
        preferred_element_type=jnp.float32,
    )
    for j in range(16):
        lanes = slice(128 * j, 128 * j + 128)
        merged = jnp.where(
            spot < 32, wide_ref[0:128, lanes],
            jnp.where(spot < 64, wide_ref[128:256, lanes], jnp.where(spot < 96, wide_ref[256:384, lanes], pieces)),
        )
        back_ref[128 * j:128 * j + 128, :] = merged.astype(jnp.bfloat16)


def score_call(orders, got, full_rows, half_rows, limit):
    vmem = pl.BlockSpec(memory_space=pltpu.VMEM)
    return pl.pallas_call(
        score_kernel,
        out_shape=jax.ShapeDtypeStruct((2048, 128), jnp.bfloat16),
        in_specs=[pl.BlockSpec(memory_space=pltpu.SMEM), vmem, vmem, vmem, vmem],
        out_specs=vmem,
        scratch_shapes=[
            pltpu.VMEM((384, 2048), jnp.bfloat16),
            pltpu.VMEM((2048, 512), jnp.bfloat16),
            pltpu.VMEM((4, 384, 128), jnp.float32),
            pltpu.VMEM((384, 512), jnp.float32),
            pltpu.VMEM((384, 2048), jnp.float32),
        ],
        compiler_params=pltpu.CompilerParams(vmem_limit_bytes=20 * 1024 * 1024),
    )(orders, got, full_rows, half_rows, limit)


def home_kernel(valid_ref, codes_ref, got_ref, waves_ref, score_ref, out_ref, mix_ref, turned_ref):
    mix_ref[...] = got_ref[...].astype(jnp.float32)
    for f in range(8):
        rows = mix_ref[pl.ds(f, 256, stride=8), :]
        if f == 0:
            spot = iota((256, 128), 1)
            pieces = jnp.where((spot >= 96) & (spot < 99), rows, 0.0)
            score_ref[0] = jnp.sum(pieces) / valid_ref[0]
        turned = jnp.transpose(rows, (1, 0)).astype(jnp.bfloat16)
        for w in range(3):
            turned_ref[w, 32 * f:32 * f + 32, :] = turned[32 * w:32 * w + 32]
    full, even, odd, _ = picks(codes_ref[0:1, :], codes_ref[1:2, :])
    first = dot(turned_ref[0], full) + dot(turned_ref[2], even)
    second = dot(turned_ref[1], full) + dot(turned_ref[2], odd)
    natural = jnp.concatenate([first, second], axis=1).astype(jnp.bfloat16)
    out_ref[...] = dot(natural, waves_ref[...]).astype(jnp.bfloat16)


def home_call(valid, codes, got, waves):
    vmem = pl.BlockSpec(memory_space=pltpu.VMEM)
    smem = pl.BlockSpec(memory_space=pltpu.SMEM)
    return pl.pallas_call(
        home_kernel,
        out_shape=(
            jax.ShapeDtypeStruct((1,), jnp.float32),
            jax.ShapeDtypeStruct((256, waves.shape[1]), jnp.bfloat16),
        ),
        in_specs=[smem, vmem, vmem, vmem],
        out_specs=(smem, vmem),
        scratch_shapes=[pltpu.VMEM((2048, 128), jnp.float32), pltpu.VMEM((3, 256, 256), jnp.bfloat16)],
        compiler_params=pltpu.CompilerParams(vmem_limit_bytes=20 * 1024 * 1024),
    )(valid, codes, got, waves)


def exchange(rows):
    return lax.all_to_all(rows, both_axes, split_axis=0, concat_axis=0, tiled=True)


def shift_of(order):
    return jnp.where(order >= 368, 0, (368 - order + 31) // 32 * 32)


def ranked(orders):
    rank = jnp.sum((orders[..., None] > orders[..., None, :]).astype(jnp.int32), axis=-1)
    return rank


def exact(equation, left, right):
    return jnp.einsum(equation, left, right, preferred_element_type=jnp.float32).astype(jnp.bfloat16)


def unpacked(grid, legendre, target, owner, cutoff, waves, modes_valid):
    fields, rows = grid.shape[1:3]
    modes, levels = legendre.shape[1:]
    e = lax.axis_index("ens")
    j = lax.axis_index("lat")
    natural = jnp.arange(modes, dtype=jnp.int32)
    place = jnp.arange(256, dtype=jnp.int32)
    full_slots = place // 16 * 24 + place % 16
    half_slots = place // 16 * 24 + 16 + place % 16 // 2
    pick_full = (owner[full_slots][:, None] == natural).astype(jnp.bfloat16)
    pick_half = (owner[half_slots][:, None] == natural).astype(jnp.bfloat16)
    zeros = jnp.zeros_like(pick_full)
    odd = (place % 2 == 1)[:, None]
    pick = jnp.stack([
        jnp.stack([pick_full, zeros], axis=1),
        jnp.stack([zeros, pick_full], axis=1),
        jnp.stack([jnp.where(odd, zeros, pick_half), jnp.where(odd, pick_half, zeros)], axis=1),
    ], axis=1)
    table = waves.reshape(2, modes, -1)
    fourier = exact("cmn,fan->cmfa", table, grid[0])
    fourier = exchange(exact("dwcm,cmfa->dwfa", pick, fourier).reshape(256, 6, 128))
    fourier = fourier.reshape(16, 16, 3, fields, rows)
    bands = lax.dynamic_slice_in_dim(legendre, 2 * e, 2, axis=0)
    pick_orders = jnp.stack([pick_full, pick_half], axis=1)
    weights = exchange(exact("dom,rml->drol", pick_orders, bands).reshape(256, 4, levels))
    weights = weights.reshape(16, rows, 2, levels)
    weights = jnp.stack([weights[:, :, 0], weights[:, :, 0], weights[:, :, 1]], axis=2)
    coeffs = jnp.einsum("jewfa,jawl->ewfl", fourier, weights, preferred_element_type=jnp.float32)

    own = lax.dynamic_slice_in_dim(owner, 24 * j, 24)
    full_rows = lax.dynamic_index_in_dim(target, e, 0, keepdims=False)
    half_rows = lax.dynamic_slice(target, (16 + e // 2, 0, e % 2, 0), (1, fields, 1, levels))[0, :, 0]
    goal = jnp.stack([full_rows[:, 0], full_rows[:, 1], half_rows])
    order = jnp.stack([own[e], own[e], own[16 + e // 2]])[:, None, None]
    level = jnp.arange(levels, dtype=jnp.int32)
    inside = ((level >= order) & (level <= cutoff[None, :, None])).astype(jnp.float32)
    offset = delta_abs * delta_abs
    spread = coeffs[:, None] - coeffs[None]
    height = jnp.sqrt(spread * spread + offset)
    pair_value = jnp.sum(height - delta_abs, axis=1)
    pair_slope = jnp.sum(spread / height, axis=1)
    spread = coeffs - goal
    height = jnp.sqrt(spread * spread + offset)
    score = jnp.sum(inside * ((height - delta_abs) / 16.0 - pair_value / 512.0))
    grad = (inside * (spread / height - pair_slope / 16.0)).astype(jnp.bfloat16)
    score = exchange(jnp.full((256, 1, 128), score, jnp.float32))
    mean_score = (jnp.sum(score[:, 0, 0]) / modes_valid[0]).reshape(1)

    back = exchange(exact("ewfl,jawl->jewfa", grad, weights).reshape(256, 6, 128))
    back = exact("dwcm,dwfa->facm", pick, back.reshape(256, 3, fields, rows))
    return mean_score, exact("facm,cmn->fan", back, table)[None]


def body(grid, legendre, target, owner, cutoff):
    fields, rows, lon_count = grid.shape[1:]
    modes = legendre.shape[1]
    e = lax.axis_index("ens")
    j = lax.axis_index("lat")
    waves = jnp.asarray(wave_table(modes, lon_count).reshape(2 * modes, lon_count))
    sent, codes = send_call(
        e.reshape(1), owner.reshape(1, modes), grid.reshape(fields * rows, lon_count), waves, legendre
    )
    got = exchange(sent.reshape(256, 2, 896)).reshape(512, 896)

    by_lat = owner.reshape(16, 24)
    rank = ranked(by_lat)
    spots = jnp.arange(24, dtype=jnp.int32)
    by_rank = jnp.sum(jnp.where(rank[:, :, None] == spots, by_lat[:, :, None], 0), axis=1)
    long_orders = by_rank[:, 0:16:2]
    short_orders = by_rank[:, 23:15:-1]
    fits = jnp.all(360 + shift_of(short_orders) <= 511 + long_orders)

    own = lax.dynamic_slice_in_dim(owner, 24 * j, 24)
    own_rank = ranked(own)
    is_full = own_rank == e
    is_half = own_rank == 23 - e // 2
    full_order = jnp.sum(jnp.where(is_full, own, 0))
    half_order = jnp.sum(jnp.where(is_half, own, 0))
    shift = shift_of(half_order)
    orders = jnp.stack([full_order, half_order, shift])
    full_slot = jnp.sum(jnp.where(is_full, spots, 0))
    half_slot = jnp.sum(jnp.where(is_half, spots, 0))
    full_rows = lax.dynamic_index_in_dim(target, full_slot, 0, keepdims=False)
    full_rows = jnp.concatenate([full_rows[:, 0], full_rows[:, 1]])
    half_rows = lax.dynamic_slice(target, (half_slot, 0, e % 2, 0), (1, fields, 1, target.shape[3]))
    half_rows = jnp.pad(half_rows[0, :, 0], ((0, 0), (0, 512 - target.shape[3])))
    half_rows = lax.dynamic_slice_in_dim(jnp.concatenate([half_rows, half_rows], axis=1), 512 - shift, 512, axis=1)
    limit = jnp.broadcast_to(cutoff[:, None], (fields, 128))
    cut_level = cutoff.astype(jnp.float32)
    modes_valid = jnp.sum((cut_level + 1.0) * (cut_level + 2.0)).reshape(1)

    back = score_call(orders, got, full_rows, half_rows, limit)
    home = exchange(back.reshape(256, 8, 128)).reshape(2048, 128)
    mean_score, grid_grad = home_call(modes_valid, codes, home, waves)
    grid_grad = grid_grad.reshape(1, fields, rows, lon_count)
    return lax.cond(
        fits,
        lambda: (mean_score, grid_grad),
        lambda: unpacked(grid, legendre, target, owner, cutoff, waves, modes_valid),
    )


def solution(mesh):
    in_specs = (
        P("ens", None, "lat", None),
        P("lat", None, None),
        P("lat", None, None, None),
        P(),
        P(),
    )
    out_specs = (P(), P("ens", None, "lat", None))
    return jax.shard_map(body, mesh=mesh, in_specs=in_specs, out_specs=out_specs, check_vma=False)
```

time: 101 us -> 91.7 us (0.908)
  waiting for transfers between devices: 50.7 us -> 35.8 us
  between operations: 3.32 us -> 7.66 us
  local copies, waits for them, and re-layouts: 9.21 us -> 6.44 us
  other arithmetic: 2.65 us -> 4.56 us
  Pallas kernels: 11.3 us -> 12.7 us
    all_to_all x2, waiting for transfers between devices: 50.7 us -> 35.8 us  [exchange(): lax.all_to_all(rows, both_axes, split_axis=0, concat_axis=0, tiled=True)]
    unnamed x13 -> x7, local copies, waits for them, and re-layouts: 1.69 us -> 0.02 us
    pallas_call x3, Pallas kernels: 11.3 us -> 12.7 us  [the longest x1 5.79 us: score_call(): pl.pallas_call(score_kernel, out_shape=jax.ShapeDtypeStruct((2048, 128),...]
    reduce_sum x2 -> x5, other arithmetic: 1.24 us -> 2.22 us  [the longest x1 0.79 us: body(): half_slot = jnp.sum(jnp.where(is_half, spots, 0))]
    reshape x9 -> x3, local copies, waits for them, and re-layouts: 5.3 us -> 4.45 us  [the longest x2 3.77 us: body(): got = exchange(sent.reshape(256, 2, 896)).reshape(512, 896)]
  transfers between devices with their start and end apart: 2 -> 2, of which waited for: 2 -> 2; matrix products, arithmetic and copies ran while one was open for 3% -> 7% of each run, Pallas kernels for 0% -> 0%
where the time goes in v1:
time: 91.7 us; the launch traced here: 91.2 us
  waiting for transfers between devices  35.8 us (39%)
  starting transfers between devices  23.2 us (25%)
  Pallas kernels  12.7 us (14%)
  between operations  7.66 us (8%)
  local copies, waits for them, and re-layouts  6.44 us (7%)
  other arithmetic  4.56 us (5%)
    all_to_all x2, waiting for transfers between devices, exchange(): lax.all_to_all(rows, both_axes, split_axis=0, concat_axis=0, tiled=True)  35.8 us
    all_to_all x2, starting transfers between devices, exchange(): lax.all_to_all(rows, both_axes, split_axis=0, concat_axis=0, tiled=True)  23.2 us
    pallas_call x1, Pallas kernels, score_call(): pl.pallas_call(score_kernel, out_shape=jax.ShapeDtypeStruct((2048, 128),...  5.79 us
    pallas_call x1, Pallas kernels, send_call(): pl.pallas_call(send_kernel, out_shape=(jax.ShapeDtypeStruct((512, 896), j...  4.05 us
    reshape x2, local copies, waits for them, and re-layouts, body(): got = exchange(sent.reshape(256, 2, 896)).reshape(512, 896)  3.77 us
    pallas_call x1, Pallas kernels, home_call(): pl.pallas_call(home_kernel, out_shape=(jax.ShapeDtypeStruct((1,), jnp.flo...  2.82 us
  transfers between devices with their start and end apart: 2, of which 2 were waited for; matrix products, arithmetic and copies ran while one was open for 7% of the time, Pallas kernels for 0%

profile of v1, /device:TPU:1, one launch (start us, length us, event | category | flops | bytes accessed | tf_op | source)
XLA Modules:
  0.0 91.2 jit_solution(11711351328593485424)
XLA Ops:
  0.6 0.7 reshape.387.owner_ref
  1.3 4.1 %shard_map.81 = (bf16[512,896]{1,0:T(8,128)(2,1)S(1)}, f32[8,384]{1,0:T(8,128)S(1)}) custom-call(s32[1]{0:T(128)} %bitcast.47.place_ref, s32[1,384]{1,0:T(1,128)S(1)} %reshape.387.owner_ref, bf16[256,1440]{1,0:T(8,128)(2,1)} %bitcast.126, bf16[768,1440]{1,0:T(8,128)(2,1)} %constant.215.clone.waves_hbm.waves_ref, bf16[32,384,384]{2,1,0:T(8,128)(2,1)} %legendre_hbm.1), custom_call_target="tpu_custom_call" | custom-call | tf_op jit(solution)/shard_map/pallas_call | solution.py:121
  5.4 0.0 copy-start
  5.4 1.3 %reshape.389 = bf16[256,2,896]{2,1,0:T(2,128)(2,1)} reshape(bf16[512,896]{1,0:T(8,128)(2,1)S(1)} %get-tuple-element.37) | data formatting | bytes 1835008 | tf_op jit(solution)/shard_map/reshape | solution.py:370
  6.7 0.0 copy-start.6
  6.7 16.5 %all-to-all-start.4 = ((bf16[256,2,896]{2,1,0:T(2,128)(2,1)}), bf16[256,2,896]{2,1,0:T(2,128)(2,1)}, u32[]{:S(2)}, u32[]{:S(2)}) async-start(bf16[256,2,896]{2,1,0:T(2,128)(2,1)} %reshape.389), calls=%async_computation.4 | async-start | bytes 1835008 | tf_op jit(solution)/shard_map/all_to_all | solution.py:292
  23.3 0.0 copy-done
  23.3 0.1 dynamic_slice.34
  23.4 0.2 convert_reduce_fusion.1
  23.5 0.8 fusion.63
  28.8 0.8 constant_dynamic-slice_fusion
  30.2 0.7 constant_dynamic-slice_fusion.1
  30.9 0.0 copy-start.1
  31.0 1.6 %pad_add_fusion.1.orders_ref = s32[3]{0:T(128)S(1)} fusion(s32[1]{0:T(128)} %bitcast.51, s32[1]{0:T(128)} %bitcast.50, s32[1]{0:T(128)} %bitcast.49), kind=kLoop, calls=%fused_computation.126 | loop fusion | flops 6 | bytes 24 | tf_op jit(solution)/shard_map/stack | solution.py:387
  32.6 0.1 fusion.52.half_ref
  32.7 17.9 %all-to-all-done.4 = bf16[256,2,896]{2,1,0:T(2,128)(2,1)} async-done(((bf16[256,2,896]{2,1,0:T(2,128)(2,1)}), bf16[256,2,896]{2,1,0:T(2,128)(2,1)}, u32[]{:S(2)}, u32[]{:S(2)}) %all-to-all-start.4) | async-done | bytes 917536 | tf_op jit(solution)/shard_map/all_to_all | solution.py:292
  50.6 2.5 %reshape.390.got_ref = bf16[512,896]{1,0:T(8,128)(2,1)S(1)} reshape(bf16[256,2,896]{2,1,0:T(2,128)(2,1)} %all-to-all-done.4) | data formatting | bytes 1835008 | tf_op jit(solution)/shard_map/reshape | solution.py:370
  53.0 0.0 copy-done.6
  53.1 0.1 broadcast_in_dim.43.cutoff_ref
  53.1 5.8 %shard_map.82 = bf16[2048,128]{1,0:T(8,128)(2,1)} custom-call(s32[3]{0:T(128)S(1)} %pad_add_fusion.1.orders_ref, bf16[512,896]{1,0:T(8,128)(2,1)S(1)} %reshape.390.got_ref, f32[16,384]{1,0:T(8,128)S(1)} %pad_maximum_fusion.6.full_ref, f32[8,512]{1,0:T(8,128)S(1)} %fusion.52.half_ref, s32[8,128]{1,0:T(8,128)S(1)} %broadcast_in_dim.43.cutoff_ref), custom_call_target="tpu_custom_call" | custom-call | tf_op jit(solution)/shard_map/pallas_call | solution.py:241
  58.9 6.7 %all-to-all-start.5 = ((bf16[256,8,128]{2,1,0:T(8,128)(2,1)}), bf16[256,8,128]{2,1,0:T(8,128)(2,1)S(1)}, u32[]{:S(2)}, u32[]{:S(2)}) async-start(bf16[256,8,128]{2,1,0:T(8,128)(2,1)} %bitcast.56), calls=%async_computation.5 | async-start | bytes 1048576 | tf_op jit(solution)/shard_map/all_to_all | solution.py:292
  65.6 0.1 gt.28
  65.7 0.4 convert_reduce_fusion
  66.1 0.2 select_reduce_fusion
  66.3 0.1 slice.39
  66.4 0.1 slice.28
  66.5 0.1 rev.3
  66.5 0.7 fusion.59
  67.8 0.6 multiply_reduce_fusion
  68.5 17.8 %all-to-all-done.5 = bf16[256,8,128]{2,1,0:T(8,128)(2,1)S(1)} async-done(((bf16[256,8,128]{2,1,0:T(8,128)(2,1)}), bf16[256,8,128]{2,1,0:T(8,128)(2,1)S(1)}, u32[]{:S(2)}, u32[]{:S(2)}) %all-to-all-start.5) | async-done | bytes 524320 | tf_op jit(solution)/shard_map/all_to_all | solution.py:292
  86.3 0.0 copy-done.1
  86.3 2.8 %shard_map.83 = (f32[1]{0:T(128)}, bf16[256,1440]{1,0:T(8,128)(2,1)}) custom-call(f32[1]{0:T(128)} %bitcast.46.valid_ref, f32[8,384]{1,0:T(8,128)S(1)} %get-tuple-element.36.codes_ref, bf16[2048,128]{1,0:T(8,128)(2,1)S(1)} %bitcast.122, bf16[768,1440]{1,0:T(8,128)(2,1)S(1)} %copy-done.1), custom_call_target="tpu_custom_call" | custom-call | tf_op jit(solution)/shard_map/pallas_call | solution.py:278
  89.1 0.9 conditional.1
  (5 shorter events, 0.0 us)
Async XLA Ops:
  5.4 17.9 %copy-start = (s32[384]{0:T(512)S(1)}, s32[384]{0:T(512)}, u32[]{:S(2)}) copy-start(s32[384]{0:T(512)} %param.11) | copy-start | bytes 4612
  6.7 46.3 %copy-start.6 = (s32[8]{0:T(128)S(1)}, s32[8]{0:T(128)}, u32[]{:S(2)}) copy-start(s32[8]{0:T(128)} %param.12) | copy-start | bytes 100
  6.7 43.9 %all-to-all-start.4 = ((bf16[256,2,896]{2,1,0:T(2,128)(2,1)}), bf16[256,2,896]{2,1,0:T(2,128)(2,1)}, u32[]{:S(2)}, u32[]{:S(2)}) async-start(bf16[256,2,896]{2,1,0:T(2,128)(2,1)} %reshape.389), calls=%async_computation.4 | async-start | bytes 1835008 | tf_op jit(solution)/shard_map/all_to_all | solution.py:292
  30.9 55.4 %copy-start.1 = (bf16[768,1440]{1,0:T(8,128)(2,1)S(1)}, bf16[768,1440]{1,0:T(8,128)(2,1)}, u32[]{:S(2)}) copy-start(bf16[768,1440]{1,0:T(8,128)(2,1)} %constant.215.clone.waves_hbm.waves_ref) | copy-start | bytes 6635524
  58.9 27.4 %all-to-all-start.5 = ((bf16[256,8,128]{2,1,0:T(8,128)(2,1)}), bf16[256,8,128]{2,1,0:T(8,128)(2,1)S(1)}, u32[]{:S(2)}, u32[]{:S(2)}) async-start(bf16[256,8,128]{2,1,0:T(8,128)(2,1)} %bitcast.56), calls=%async_computation.5 | async-start | bytes 1048576 | tf_op jit(solution)/shard_map/all_to_all | solution.py:292

commit v2 on v1

--- a/solution.py
+++ b/solution.py
@@ -34,8 +34,8 @@
 
 
 def send_kernel(
-    place_ref, owner_ref, grid_hbm, waves_hbm, legendre_hbm, out_ref, codes_ref,
-    grid_ref, waves_ref, bands_ref, table_ref, four_ref, mix_ref, sems,
+    place_ref, owner_hbm, grid_hbm, waves_hbm, legendre_hbm, out_ref, codes_ref,
+    owner_ref, grid_ref, waves_ref, bands_ref, table_ref, four_ref, mix_ref, sems,
 ):
     grid_copy = pltpu.make_async_copy(grid_hbm, grid_ref, sems.at[0])
     band_copy = pltpu.make_async_copy(
@@ -43,16 +43,19 @@
     )
     wave_copies = [
         pltpu.make_async_copy(
-            waves_hbm.at[pl.ds(384 * c, 384)], waves_ref.at[pl.ds(384 * c, 384)], sems.at[2 + c]
+            waves_hbm.at[:, pl.ds(384 * c, 384)], waves_ref.at[:, pl.ds(384 * c, 384)], sems.at[2 + c]
         )
         for c in range(2)
     ]
+    owner_copy = pltpu.make_async_copy(owner_hbm, owner_ref, sems.at[4])
+    owner_copy.start()
     band_copy.start()
     grid_copy.start()
     for copy in wave_copies:
         copy.start()
 
-    line = jnp.broadcast_to(owner_ref[...].astype(jnp.float32), (128, 384))
+    owner_copy.wait()
+    line = jnp.broadcast_to(owner_ref[...].reshape(1, 384).astype(jnp.float32), (128, 384))
     column = jnp.transpose(line, (1, 0))
     lane = iota((384, 128), 1).astype(jnp.float32)
     held = jnp.concatenate([flag(column == lane + 128.0 * t) for t in range(3)], axis=1)
@@ -89,21 +92,25 @@
         for t in range(4):
             mix_ref[3 + t, pl.ds(r, 256, stride=2), :] = packed[:, 128 * t:128 * t + 128]
 
+    for t in range(3, 7):
+        out_ref[:, :, 128 * t:128 * t + 128] = mix_ref[t].astype(jnp.bfloat16).reshape(256, 2, 128)
+
+    dims = (((1,), (1,)), ((), ()))
     grid_copy.wait()
     for c in range(2):
         wave_copies[c].wait()
-        four_ref[384 * c:384 * c + 384, :] = lax.dot_general(
-            waves_ref[384 * c:384 * c + 384, :], grid_ref[...], (((1,), (1,)), ((), ())),
-            preferred_element_type=jnp.float32,
-        ).astype(jnp.bfloat16)
-        part = dot(full, four_ref[384 * c:384 * c + 384, :])
+        columns = slice(384 * c, 384 * c + 384)
+        four_ref[:, columns] = dot(grid_ref[...], waves_ref[:, columns]).astype(jnp.bfloat16)
+        part = lax.dot_general(full, four_ref[:, columns], dims, preferred_element_type=jnp.float32)
         for h in range(2):
             mix_ref[h, pl.ds(c, 256, stride=2), :] = part[:, 128 * h:128 * h + 128]
-    part = dot(jnp.concatenate([even, odd], axis=1), four_ref[...])
+    part = lax.dot_general(
+        jnp.concatenate([even, odd], axis=1), four_ref[...], dims, preferred_element_type=jnp.float32
+    )
     for h in range(2):
         mix_ref[2, pl.ds(h, 256, stride=2), :] = part[:, 128 * h:128 * h + 128]
-    for t in range(7):
-        out_ref[:, 128 * t:128 * t + 128] = mix_ref[t].astype(jnp.bfloat16)
+    for t in range(3):
+        out_ref[:, :, 128 * t:128 * t + 128] = mix_ref[t].astype(jnp.bfloat16).reshape(256, 2, 128)
 
 
 def picks(full_code, half_code):
@@ -121,41 +128,46 @@
     return pl.pallas_call(
         send_kernel,
         out_shape=(
-            jax.ShapeDtypeStruct((512, 896), jnp.bfloat16),
+            jax.ShapeDtypeStruct((256, 2, 896), jnp.bfloat16),
             jax.ShapeDtypeStruct((8, 384), jnp.float32),
         ),
-        in_specs=[pl.BlockSpec(memory_space=pltpu.SMEM), vmem, anywhere, anywhere, anywhere],
+        in_specs=[pl.BlockSpec(memory_space=pltpu.SMEM), anywhere, anywhere, anywhere, anywhere],
         out_specs=(vmem, vmem),
         scratch_shapes=[
+            pltpu.VMEM((384,), jnp.int32),
             pltpu.VMEM((256, 1440), jnp.bfloat16),
-            pltpu.VMEM((768, 1440), jnp.bfloat16),
+            pltpu.VMEM((1440, 768), jnp.bfloat16),
             pltpu.VMEM((2, 384, 384), jnp.bfloat16),
             pltpu.VMEM((768, 512), jnp.bfloat16),
-            pltpu.VMEM((768, 256), jnp.bfloat16),
+            pltpu.VMEM((256, 768), jnp.bfloat16),
             pltpu.VMEM((7, 512, 128), jnp.float32),
-            pltpu.SemaphoreType.DMA((4,)),
+            pltpu.SemaphoreType.DMA((5,)),
         ],
-        compiler_params=pltpu.CompilerParams(vmem_limit_bytes=20 * 1024 * 1024),
+        compiler_params=pltpu.CompilerParams(vmem_limit_bytes=58 * 1024 * 1024),
     )(place, owner, grid, waves, legendre)
 
 
 def score_kernel(
     orders_ref, got_ref, full_ref, half_ref, cutoff_ref, back_ref,
-    rows_ref, tiled_ref, coeffs_ref, grads_ref, wide_ref,
+    flat_ref, rows_ref, coeffs_ref, grads_ref, total_ref,
 ):
-    lane_field = iota((32, 128), 1) // 32
-    for j in range(16):
-        for q in range(3):
-            block = got_ref[32 * j:32 * j + 32, 128 * q:128 * q + 128]
+    flat_ref[...] = got_ref[...].reshape(512, 896)
+    lane_group = iota((32, 128), 1) // 32
+    for q in range(3):
+        for group in range(4):
+            blocks = [
+                flat_ref[128 * group + 32 * i:128 * group + 32 * i + 32, 128 * q:128 * q + 128].astype(jnp.float32)
+                for i in range(4)
+            ]
             for k in range(4):
+                merged = jnp.zeros((32, 128), jnp.float32)
+                for i in range(4):
+                    turn = (i - k) % 4
+                    block = pltpu.roll(blocks[i], 32 * turn, 1) if turn else blocks[i]
+                    merged = jnp.where(lane_group == i, block, merged)
                 row = (q * 4 + k) * 32
-                rows_ref[row:row + 32, 128 * j:128 * j + 128] = jnp.where(
-                    lane_field == k, block, jnp.zeros_like(block)
-                )
-        band = got_ref[32 * j:32 * j + 32, 384:896]
-        for k in range(4):
-            tiled_ref[128 * j + 32 * k:128 * j + 32 * k + 32, :] = band
-    coeffs = dot(rows_ref[...], tiled_ref[...])
+                rows_ref[row:row + 32, 128 * group:128 * group + 128] = merged.astype(jnp.bfloat16)
+    coeffs = dot(rows_ref[...], flat_ref[:, 384:896])
     for t in range(4):
         coeffs_ref[t] = coeffs[:, 128 * t:128 * t + 128]
     offset = delta_abs * delta_abs
@@ -165,16 +177,18 @@
         inside = (level >= order) & (level <= limit)
         member = [load(e) for e in range(16)]
         slope = [jnp.zeros((8, 128), jnp.float32) for _ in range(16)]
-        pair_value = jnp.zeros((8, 128), jnp.float32)
+        rest = jnp.zeros((8, 128), jnp.float32)
         for i in range(16):
             for k in range(i + 1, 16):
                 spread = member[i] - member[k]
-                square = spread * spread + offset
-                inverse = lax.rsqrt(square)
+                inverse = lax.rsqrt(spread * spread + offset)
                 step_slope = spread * inverse
                 slope[i] = slope[i] + step_slope
                 slope[k] = slope[k] - step_slope
-                pair_value = pair_value + (square * inverse - delta_abs)
+                rest = rest + (inverse - 1.0 / delta_abs)
+        pair_value = offset * rest
+        for i in range(1, 16):
+            pair_value = pair_value + (member[i] - member[0]) * slope[i]
         own_value = jnp.zeros((8, 128), jnp.float32)
         for i in range(16):
             spread = member[i] - goal
@@ -182,12 +196,18 @@
             inverse = lax.rsqrt(square)
             own_value = own_value + (square * inverse - delta_abs)
             store(i, jnp.where(inside, spread * inverse - slope[i] / 16.0, 0.0))
-        return jnp.where(inside, own_value / 16.0 - pair_value / 256.0, 0.0)
-
-    def full_column(step, total):
+        total_ref[...] += jnp.where(inside, own_value / 16.0 - pair_value / 256.0, 0.0)
+
+    total_ref[...] = jnp.zeros((8, 128), jnp.float32)
+    full_order, half_order, shift, highest = [orders_ref[i] for i in range(4)]
+
+    @pl.loop(0, 6)
+    def _(step):
         part = step // 3
         third = step % 3
         lanes = pl.ds(pl.multiple_of(third * 128, 128), 128)
+        first = third * 128
+        active = (first + 127 >= full_order) & (first <= highest)
 
         def load(e):
             return coeffs_ref[third, pl.ds(2 * e + part, 8, stride=32), :]
@@ -195,11 +215,21 @@
         def store(e, value):
             grads_ref[pl.ds(pl.multiple_of(part * 128 + 8 * e, 8), 8), lanes] = value
 
-        goal = full_ref[pl.ds(pl.multiple_of(part * 8, 8), 8), lanes]
-        return total + column(iota((8, 128), 1) + third * 128, orders_ref[0], goal, load, store)
-
-    def half_column(tile, total):
+        @pl.when(active)
+        def _():
+            goal = full_ref[pl.ds(pl.multiple_of(part * 8, 8), 8), lanes]
+            column(iota((8, 128), 1) + first, full_order, goal, load, store)
+
+        @pl.when(jnp.logical_not(active))
+        def _():
+            grads_ref[pl.ds(pl.multiple_of(part * 128, 128), 128), lanes] = jnp.zeros((128, 128), jnp.float32)
+
+    @pl.loop(0, 4)
+    def _(tile):
         lanes = pl.ds(pl.multiple_of(tile * 128, 128), 128)
+        first = tile * 128 - shift
+        first = jnp.where(first < 0, first + 512, first)
+        active = ((first + 127 >= half_order) & (first <= highest)) | (first - 385 >= half_order)
 
         def load(e):
             return jnp.concatenate(
@@ -209,13 +239,18 @@
         def store(e, value):
             grads_ref[256 + 8 * e:256 + 8 * e + 8, lanes] = value
 
-        level = iota((8, 128), 1) + tile * 128 - orders_ref[2]
-        level = jnp.where(level < 0, level + 512, level)
-        return total + column(level, orders_ref[1], half_ref[:, lanes], load, store)
-
-    total = lax.fori_loop(0, 6, full_column, jnp.zeros((8, 128), jnp.float32))
-    total = lax.fori_loop(0, 4, half_column, total)
+        @pl.when(active)
+        def _():
+            level = iota((8, 128), 1) + first
+            level = jnp.where(level >= 512, level - 512, level)
+            column(level, half_order, half_ref[:, lanes], load, store)
+
+        @pl.when(jnp.logical_not(active))
+        def _():
+            grads_ref[256:384, lanes] = jnp.zeros((128, 128), jnp.float32)
+
     grads_ref[0:256, 384:512] = jnp.zeros((256, 128), jnp.float32)
+    total = total_ref[...]
     score = jnp.sum(jnp.sum(total, axis=1, keepdims=True), axis=0, keepdims=True)
     high = score.astype(jnp.bfloat16).astype(jnp.float32)
     middle = (score - high).astype(jnp.bfloat16).astype(jnp.float32)
@@ -223,16 +258,18 @@
     spot = iota((128, 128), 1)
     pieces = jnp.where(spot == 96, high, jnp.where(spot == 97, middle, jnp.where(spot == 98, low, 0.0)))
 
-    wide_ref[...] = lax.dot_general(
-        grads_ref[...].astype(jnp.bfloat16), tiled_ref[...], (((1,), (1,)), ((), ())),
+    waves_grad = lax.dot_general(
+        grads_ref[...].astype(jnp.bfloat16), flat_ref[:, 384:896], (((1,), (1,)), ((), ())),
         preferred_element_type=jnp.float32,
     )
     for j in range(16):
-        lanes = slice(128 * j, 128 * j + 128)
-        merged = jnp.where(
-            spot < 32, wide_ref[0:128, lanes],
-            jnp.where(spot < 64, wide_ref[128:256, lanes], jnp.where(spot < 96, wide_ref[256:384, lanes], pieces)),
-        )
+        merged = pieces
+        for w in range(3):
+            block = waves_grad[128 * w:128 * w + 128, 128 * (j // 4):128 * (j // 4) + 128]
+            turn = (w - j) % 4
+            if turn:
+                block = pltpu.roll(block, 32 * turn, 1)
+            merged = jnp.where(spot // 32 == w, block, merged)
         back_ref[128 * j:128 * j + 128, :] = merged.astype(jnp.bfloat16)
 
 
@@ -244,11 +281,11 @@
         in_specs=[pl.BlockSpec(memory_space=pltpu.SMEM), vmem, vmem, vmem, vmem],
         out_specs=vmem,
         scratch_shapes=[
-            pltpu.VMEM((384, 2048), jnp.bfloat16),
-            pltpu.VMEM((2048, 512), jnp.bfloat16),
+            pltpu.VMEM((512, 896), jnp.bfloat16),
+            pltpu.VMEM((384, 512), jnp.bfloat16),
             pltpu.VMEM((4, 384, 128), jnp.float32),
             pltpu.VMEM((384, 512), jnp.float32),
-            pltpu.VMEM((384, 2048), jnp.float32),
+            pltpu.VMEM((8, 128), jnp.float32),
         ],
         compiler_params=pltpu.CompilerParams(vmem_limit_bytes=20 * 1024 * 1024),
     )(orders, got, full_rows, half_rows, limit)
@@ -363,11 +400,13 @@
     modes = legendre.shape[1]
     e = lax.axis_index("ens")
     j = lax.axis_index("lat")
-    waves = jnp.asarray(wave_table(modes, lon_count).reshape(2 * modes, lon_count))
+    table = wave_table(modes, lon_count).reshape(2 * modes, lon_count)
+    waves = jnp.asarray(table)
+    turned = jnp.asarray(np.ascontiguousarray(table.T))
     sent, codes = send_call(
-        e.reshape(1), owner.reshape(1, modes), grid.reshape(fields * rows, lon_count), waves, legendre
-    )
-    got = exchange(sent.reshape(256, 2, 896)).reshape(512, 896)
+        e.reshape(1), owner, grid.reshape(fields * rows, lon_count), turned, legendre
+    )
+    got = exchange(sent)
 
     by_lat = owner.reshape(16, 24)
     rank = ranked(by_lat)
@@ -384,7 +423,7 @@
     full_order = jnp.sum(jnp.where(is_full, own, 0))
     half_order = jnp.sum(jnp.where(is_half, own, 0))
     shift = shift_of(half_order)
-    orders = jnp.stack([full_order, half_order, shift])
+    orders = jnp.stack([full_order, half_order, shift, jnp.max(cutoff)])
     full_slot = jnp.sum(jnp.where(is_full, spots, 0))
     half_slot = jnp.sum(jnp.where(is_half, spots, 0))
     full_rows = lax.dynamic_index_in_dim(target, full_slot, 0, keepdims=False)

time: 91.7 us -> 86.3 us (0.941)
  local copies, waits for them, and re-layouts: 6.44 us -> 1.99 us
  starting transfers between devices: 23.2 us -> 22.1 us
  other arithmetic: 4.56 us -> 5.54 us
    reshape x3 -> x0, local copies, waits for them, and re-layouts: 4.45 us -> none  [the longest x2 3.77 us: body(): got = exchange(sent.reshape(256, 2, 896)).reshape(512, 896)]
    pallas_call x1, Pallas kernels: 5.79 us -> 4.41 us  [score_call(): pl.pallas_call(score_kernel, out_shape=jax.ShapeDtypeStruct((2048, 128),...]
    all_to_all x2, starting transfers between devices: 23.2 us -> 22.1 us  [exchange(): lax.all_to_all(rows, both_axes, split_axis=0, concat_axis=0, tiled=True)]
    pallas_call x1, Pallas kernels: 4.05 us -> 4.98 us  [send_call(): pl.pallas_call(send_kernel, out_shape=(jax.ShapeDtypeStruct((256, 2, 896)...]
  transfers between devices with their start and end apart: 2 -> 2, of which waited for: 2 -> 2; matrix products, arithmetic and copies ran while one was open for 7% -> 9% of each run, Pallas kernels for 0% -> 0%
where the time goes in v2:
time: 86.3 us; the launch traced here: 85.9 us
  waiting for transfers between devices  35.4 us (41%)
  starting transfers between devices  22.1 us (26%)
  Pallas kernels  12.2 us (14%)
  between operations  7.82 us (9%)
  other arithmetic  5.54 us (6%)
  local copies, waits for them, and re-layouts  1.99 us (2%)
  loops' own time  0.88 us (1%)
    all_to_all x2, waiting for transfers between devices, exchange(): lax.all_to_all(rows, both_axes, split_axis=0, concat_axis=0, tiled=True)  35.4 us
    all_to_all x2, starting transfers between devices, exchange(): lax.all_to_all(rows, both_axes, split_axis=0, concat_axis=0, tiled=True)  22.1 us
    pallas_call x1, Pallas kernels, send_call(): pl.pallas_call(send_kernel, out_shape=(jax.ShapeDtypeStruct((256, 2, 896)...  4.98 us
    pallas_call x1, Pallas kernels, score_call(): pl.pallas_call(score_kernel, out_shape=jax.ShapeDtypeStruct((2048, 128),...  4.41 us
    pallas_call x1, Pallas kernels, home_call(): pl.pallas_call(home_kernel, out_shape=(jax.ShapeDtypeStruct((1,), jnp.flo...  2.78 us
    another operation x1, other arithmetic, body(): orders = jnp.stack([full_order, half_order, shift, jnp.max(cutoff)])  1.98 us
  transfers between devices with their start and end apart: 2, of which 2 were waited for; matrix products, arithmetic and copies ran while one was open for 9% of the time, Pallas kernels for 0%

profile of v2, /device:TPU:1, one launch (start us, length us, event | category | flops | bytes accessed | tf_op | source)
XLA Modules:
  0.0 85.9 jit_solution(14011688844173550004)
XLA Ops:
  0.6 0.0 copy-start.1
  0.6 0.0 copy-start.10
  0.7 5.0 %shard_map.90 = (bf16[256,2,896]{2,1,0:T(2,128)(2,1)}, f32[8,384]{1,0:T(8,128)}) custom-call(s32[1]{0:T(128)} %bitcast.47.place_ref, s32[384]{0:T(512)} %owner_hbm.1, bf16[256,1440]{1,0:T(8,128)(2,1)} %bitcast.127, bf16[1440,768]{1,0:T(8,128)(2,1)} %constant.220.clone.waves_hbm, bf16[32,384,384]{2,1,0:T(8,128)(2,1)} %legendre_hbm.1), custom_call_target="tpu_custom_call" | custom-call | tf_op jit(solution)/shard_map/pallas_call | solution.py:128
  5.6 0.0 copy-start
  5.7 0.0 copy-start.2
  5.7 15.7 %all-to-all-start.4 = ((bf16[256,2,896]{2,1,0:T(2,128)(2,1)}), bf16[256,2,896]{2,1,0:T(2,128)(2,1)S(1)}, u32[]{:S(2)}, u32[]{:S(2)}) async-start(bf16[256,2,896]{2,1,0:T(2,128)(2,1)} %get-tuple-element.37), calls=%async_computation.4 | async-start | bytes 1835008 | tf_op jit(solution)/shard_map/all_to_all | solution.py:329
  21.4 0.0 copy-done.1
  21.4 0.1 dynamic_slice.34
  21.4 0.2 convert_reduce_fusion.1
  21.6 0.8 fusion.63
  27.0 0.8 constant_dynamic-slice_fusion
  28.4 0.7 constant_dynamic-slice_fusion.1
  29.2 0.0 copy-done.10
  29.2 0.6 reduce_max.9
  29.8 2.0 %pad_add_fusion.1.orders_ref = s32[4]{0:T(128)S(1)} fusion(s32[1]{0:T(128)} %bitcast.52, s32[1]{0:T(128)} %bitcast.51, s32[1]{0:T(128)} %bitcast.50, s32[1]{0:T(128)} %bitcast.49), kind=kLoop, calls=%fused_computation.126 | loop fusion | flops 12 | bytes 32 | tf_op jit(solution)/shard_map/stack | solution.py:426
  31.8 0.1 fusion.52.half_ref
  31.9 17.5 %all-to-all-done.4.got_ref = bf16[256,2,896]{2,1,0:T(2,128)(2,1)S(1)} async-done(((bf16[256,2,896]{2,1,0:T(2,128)(2,1)}), bf16[256,2,896]{2,1,0:T(2,128)(2,1)S(1)}, u32[]{:S(2)}, u32[]{:S(2)}) %all-to-all-start.4) | async-done | bytes 917536 | tf_op jit(solution)/shard_map/all_to_all | solution.py:329
  49.4 0.1 broadcast_in_dim.43.cutoff_ref
  49.5 4.4 %shard_map.91 = bf16[2048,128]{1,0:T(8,128)(2,1)} custom-call(s32[4]{0:T(128)S(1)} %pad_add_fusion.1.orders_ref, bf16[256,2,896]{2,1,0:T(2,128)(2,1)S(1)} %all-to-all-done.4.got_ref, f32[16,384]{1,0:T(8,128)S(1)} %pad_maximum_fusion.6.full_ref, f32[8,512]{1,0:T(8,128)S(1)} %fusion.52.half_ref, s32[8,128]{1,0:T(8,128)S(1)} %broadcast_in_dim.43.cutoff_ref), custom_call_target="tpu_custom_call" | custom-call | tf_op jit(solution)/shard_map/pallas_call | solution.py:278
  53.9 6.5 %all-to-all-start.5 = ((bf16[256,8,128]{2,1,0:T(8,128)(2,1)}), bf16[256,8,128]{2,1,0:T(8,128)(2,1)S(1)}, u32[]{:S(2)}, u32[]{:S(2)}) async-start(bf16[256,8,128]{2,1,0:T(8,128)(2,1)} %bitcast.57), calls=%async_computation.5 | async-start | bytes 1048576 | tf_op jit(solution)/shard_map/all_to_all | solution.py:329
  60.4 0.1 gt.28
  60.5 0.4 convert_reduce_fusion
  60.9 0.2 select_reduce_fusion
  61.1 0.1 slice.39
  61.2 0.1 slice.28
  61.2 0.1 rev.3
  61.3 0.7 fusion.59
  62.6 0.6 multiply_reduce_fusion
  63.2 17.9 %all-to-all-done.5 = bf16[256,8,128]{2,1,0:T(8,128)(2,1)S(1)} async-done(((bf16[256,8,128]{2,1,0:T(8,128)(2,1)}), bf16[256,8,128]{2,1,0:T(8,128)(2,1)S(1)}, u32[]{:S(2)}, u32[]{:S(2)}) %all-to-all-start.5) | async-done | bytes 524320 | tf_op jit(solution)/shard_map/all_to_all | solution.py:329
  81.1 0.0 copy-done
  81.1 0.0 copy-done.2
  81.1 2.8 %shard_map.92 = (f32[1]{0:T(128)}, bf16[256,1440]{1,0:T(8,128)(2,1)}) custom-call(f32[1]{0:T(128)} %bitcast.46.valid_ref, f32[8,384]{1,0:T(8,128)S(1)} %copy-done, bf16[2048,128]{1,0:T(8,128)(2,1)S(1)} %bitcast.123, bf16[768,1440]{1,0:T(8,128)(2,1)S(1)} %copy-done.2), custom_call_target="tpu_custom_call" | custom-call | tf_op jit(solution)/shard_map/pallas_call | solution.py:315
  83.9 0.9 %conditional.1 = (f32[1]{0:T(128)}, bf16[1,8,32,1440]{3,2,1,0:T(8,128)(2,1)}) conditional(s32[]{:T(128)} %convert_element_type.77, (s32[384]{0:T(512)S(1)}, s32[8]{0:T(128)S(1)}, bf16[32,384,384]{2,1,0:T(8,128)(2,1)}, bf16[768,1440]{1,0:T(8,128)(2,1)S(1)}, bf16[1,8,32,1440]{3,2,1,0:T(8,128)(2,1)}, /*index=5*/f32[24,8,2,384]{3,2,1,0:T(2,128)}, ...), branch_computations={%region_10.15_spmd, %region_15.16_spmd} | conditional | flops 2371958272 | bytes 78532296 | solution.py:442
  (5 shorter events, 0.0 us)
Async XLA Ops:
  0.6 20.7 %copy-start.1 = (s32[384]{0:T(512)S(1)}, s32[384]{0:T(512)}, u32[]{:S(2)}) copy-start(s32[384]{0:T(512)} %owner_hbm.1) | copy-start | bytes 4612
  0.6 28.5 %copy-start.10 = (s32[8]{0:T(128)S(1)}, s32[8]{0:T(128)}, u32[]{:S(2)}) copy-start(s32[8]{0:T(128)} %param.13) | copy-start | bytes 100
  5.6 75.5 %copy-start = (f32[8,384]{1,0:T(8,128)S(1)}, f32[8,384]{1,0:T(8,128)}, u32[]{:S(2)}) copy-start(f32[8,384]{1,0:T(8,128)} %get-tuple-element.36.codes_ref) | copy-start | bytes 36868
  5.7 75.5 %copy-start.2 = (bf16[768,1440]{1,0:T(8,128)(2,1)S(1)}, bf16[768,1440]{1,0:T(8,128)(2,1)}, u32[]{:S(2)}) copy-start(bf16[768,1440]{1,0:T(8,128)(2,1)} %constant.219.clone.waves_ref) | copy-start | bytes 6635524
  5.7 43.8 %all-to-all-start.4 = ((bf16[256,2,896]{2,1,0:T(2,128)(2,1)}), bf16[256,2,896]{2,1,0:T(2,128)(2,1)S(1)}, u32[]{:S(2)}, u32[]{:S(2)}) async-start(bf16[256,2,896]{2,1,0:T(2,128)(2,1)} %get-tuple-element.37), calls=%async_computation.4 | async-start | bytes 1835008 | tf_op jit(solution)/shard_map/all_to_all | solution.py:329
  53.9 27.2 %all-to-all-start.5 = ((bf16[256,8,128]{2,1,0:T(8,128)(2,1)}), bf16[256,8,128]{2,1,0:T(8,128)(2,1)S(1)}, u32[]{:S(2)}, u32[]{:S(2)}) async-start(bf16[256,8,128]{2,1,0:T(8,128)(2,1)} %bitcast.57), calls=%async_computation.5 | async-start | bytes 1048576 | tf_op jit(solution)/shard_map/all_to_all | solution.py:329

commit v3 on v2

--- a/solution.py
+++ b/solution.py
@@ -435,15 +435,18 @@
     cut_level = cutoff.astype(jnp.float32)
     modes_valid = jnp.sum((cut_level + 1.0) * (cut_level + 2.0)).reshape(1)
 
+    flag = fits.astype(jnp.int32)
+    got, flag, modes_valid = lax.optimization_barrier((got, flag, modes_valid))
     back = score_call(orders, got, full_rows, half_rows, limit)
     home = exchange(back.reshape(256, 8, 128)).reshape(2048, 128)
     mean_score, grid_grad = home_call(modes_valid, codes, home, waves)
     grid_grad = grid_grad.reshape(1, fields, rows, lon_count)
-    return lax.cond(
-        fits,
-        lambda: (mean_score, grid_grad),
-        lambda: unpacked(grid, legendre, target, owner, cutoff, waves, modes_valid),
-    )
+    _, mean_score, grid_grad = lax.while_loop(
+        lambda state: state[0] == 0,
+        lambda state: (jnp.int32(1), *unpacked(grid, legendre, target, owner, cutoff, waves, modes_valid)),
+        (flag, mean_score, grid_grad),
+    )
+    return mean_score, grid_grad
 
 
 def solution(mesh):

time: 86.3 us -> 83.9 us (0.972)
  blocking collectives: 0 us -> 27.1 us
  waiting for transfers between devices: 35.4 us -> 12.8 us
  starting transfers between devices: 22.1 us -> 15.7 us
  local copies, waits for them, and re-layouts: 1.99 us -> 3.88 us
  between operations: 7.82 us -> 6.76 us
    all_to_all x0 -> x1, blocking collectives: none -> 27.1 us  [exchange(): lax.all_to_all(rows, both_axes, split_axis=0, concat_axis=0, tiled=True)]
    all_to_all x2 -> x1, waiting for transfers between devices: 35.4 us -> 12.8 us  [exchange(): lax.all_to_all(rows, both_axes, split_axis=0, concat_axis=0, tiled=True)]
    all_to_all x2 -> x1, starting transfers between devices: 22.1 us -> 15.7 us  [exchange(): lax.all_to_all(rows, both_axes, split_axis=0, concat_axis=0, tiled=True)]
    unnamed x9 -> x11, local copies, waits for them, and re-layouts: 0.02 us -> 1.95 us
  transfers between devices with their start and end apart: 2 -> 1, of which waited for: 2 -> 1; matrix products, arithmetic and copies ran while one was open for 9% -> 11% of each run, Pallas kernels for 0% -> 0%
where the time goes in v3:
time: 83.9 us; the launch traced here: 83.4 us
  blocking collectives  27.1 us (32%)
  starting transfers between devices  15.7 us (19%)
  waiting for transfers between devices  12.8 us (15%)
  Pallas kernels  11.4 us (14%)
  between operations  6.76 us (8%)
  other arithmetic  5.59 us (7%)
  local copies, waits for them, and re-layouts  3.88 us (5%)
    all_to_all x1, blocking collectives, exchange(): lax.all_to_all(rows, both_axes, split_axis=0, concat_axis=0, tiled=True)  27.1 us
    all_to_all x1, starting transfers between devices, exchange(): lax.all_to_all(rows, both_axes, split_axis=0, concat_axis=0, tiled=True)  15.7 us
    all_to_all x1, waiting for transfers between devices, exchange(): lax.all_to_all(rows, both_axes, split_axis=0, concat_axis=0, tiled=True)  12.8 us
    pallas_call x1, Pallas kernels, send_call(): pl.pallas_call(send_kernel, out_shape=(jax.ShapeDtypeStruct((256, 2, 896)...  4.99 us
    pallas_call x1, Pallas kernels, score_call(): pl.pallas_call(score_kernel, out_shape=jax.ShapeDtypeStruct((2048, 128),...  3.61 us
    pallas_call x1, Pallas kernels, home_call(): pl.pallas_call(home_kernel, out_shape=(jax.ShapeDtypeStruct((1,), jnp.flo...  2.84 us
    another operation x1, other arithmetic, body(): orders = jnp.stack([full_order, half_order, shift, jnp.max(cutoff)])  1.98 us
    unnamed x11, local copies, waits for them, and re-layouts  1.95 us
  transfers between devices with their start and end apart: 1, of which 1 were waited for; matrix products, arithmetic and copies ran while one was open for 11% of the time, Pallas kernels for 0%

profile of v3, /device:TPU:1, one launch (start us, length us, event | category | flops | bytes accessed | tf_op | source)
XLA Modules:
  0.0 83.4 jit_solution(11648083760935256287)
XLA Ops:
  0.6 0.0 copy-start.2
  0.6 5.0 %shard_map.86 = (bf16[256,2,896]{2,1,0:T(2,128)(2,1)}, f32[8,384]{1,0:T(8,128)}) custom-call(s32[1]{0:T(128)} %bitcast.place_ref, s32[384]{0:T(512)} %owner_hbm.1, bf16[256,1440]{1,0:T(8,128)(2,1)} %bitcast.126, bf16[1440,768]{1,0:T(8,128)(2,1)} %constant.229.clone.waves_hbm, bf16[32,384,384]{2,1,0:T(8,128)(2,1)} %legendre_hbm.1), custom_call_target="tpu_custom_call" | custom-call | tf_op jit(solution)/shard_map/pallas_call | solution.py:128
  5.6 0.0 copy-start.12
  5.7 15.7 %all-to-all-start.4 = ((bf16[256,2,896]{2,1,0:T(2,128)(2,1)}), bf16[256,2,896]{2,1,0:T(2,128)(2,1)S(1)}, u32[]{:S(2)}, u32[]{:S(2)}) async-start(bf16[256,2,896]{2,1,0:T(2,128)(2,1)} %get-tuple-element.59), calls=%async_computation.4 | async-start | bytes 1835008 | tf_op jit(solution)/shard_map/all_to_all | solution.py:329
  21.3 0.0 copy-start
  21.3 0.0 copy-start.1
  21.4 0.0 copy-done.2
  21.4 0.1 dynamic_slice.35
  21.5 0.2 convert_reduce_fusion.1
  21.6 0.8 fusion.63
  25.6 0.1 gt.28
  25.7 0.4 convert_reduce_fusion
  26.1 0.2 select_reduce_fusion
  26.3 0.1 slice.28
  26.4 0.1 slice.47
  27.1 0.1 rev.3
  27.2 0.7 fusion.59
  28.5 1.9 %copy.61 = f32[24,8,2,384]{3,1,2,0:T(8,128)} copy(f32[24,8,2,384]{3,2,1,0:T(2,128)} %param.11) | data formatting | bytes 1179648 | tf_op args[2]
  31.1 0.7 constant_dynamic-slice_fusion
  31.9 0.0 copy-done.12
  31.9 0.6 reduce_max.9
  33.1 0.7 dynamic-slice_bitcast_fusion.2
  33.8 2.0 %pad_add_fusion.1.orders_ref = s32[4]{0:T(128)S(1)} fusion(s32[1]{0:T(128)} %bitcast.6, s32[1]{0:T(128)} %bitcast.5, s32[1]{0:T(128)} %bitcast.4, s32[1]{0:T(128)} %bitcast.3), kind=kLoop, calls=%fused_computation.125 | loop fusion | flops 12 | bytes 32 | tf_op jit(solution)/shard_map/stack | solution.py:426
  35.8 0.7 multiply_reduce_fusion
  36.5 0.1 fusion.52.half_ref
  36.6 12.8 %all-to-all-done.4.got_ref = bf16[256,2,896]{2,1,0:T(2,128)(2,1)S(1)} async-done(((bf16[256,2,896]{2,1,0:T(2,128)(2,1)}), bf16[256,2,896]{2,1,0:T(2,128)(2,1)S(1)}, u32[]{:S(2)}, u32[]{:S(2)}) %all-to-all-start.4) | async-done | bytes 917536 | tf_op jit(solution)/shard_map/all_to_all | solution.py:329
  49.4 0.1 broadcast_in_dim.43.cutoff_ref
  49.5 3.6 %shard_map.87 = bf16[2048,128]{1,0:T(8,128)(2,1)S(1)} custom-call(s32[4]{0:T(128)S(1)} %pad_add_fusion.1.orders_ref, bf16[256,2,896]{2,1,0:T(2,128)(2,1)S(1)} %all-to-all-done.4.got_ref, f32[16,384]{1,0:T(8,128)S(1)} %pad_maximum_fusion.6.full_ref, f32[8,512]{1,0:T(8,128)S(1)} %fusion.52.half_ref, s32[8,128]{1,0:T(8,128)S(1)} %broadcast_in_dim.43.cutoff_ref), custom_call_target="tpu_custom_call" | custom-call | tf_op jit(solution)/shard_map/pallas_call | solution.py:278
  53.1 0.0 copy-start.10
  53.1 27.1 %all_to_all.34 = bf16[256,8,128]{2,1,0:T(8,128)(2,1)S(1)} all-to-all(bf16[256,8,128]{2,1,0:T(8,128)(2,1)S(1)} %bitcast.122), channel_id=1, replica_groups=mesh['ens'=16,'lat'=16] {'lat','ens'}, dimensions={0} | all-to-all | bytes 1048576 | tf_op jit(solution)/shard_map/all_to_all | solution.py:329
  80.2 0.0 copy-done
  80.2 0.0 copy-done.1
  80.2 2.8 %shard_map.88 = (f32[1]{0:T(128)}, bf16[256,1440]{1,0:T(8,128)(2,1)}) custom-call(f32[1]{0:T(128)} %bitcast.2.valid_ref, f32[8,384]{1,0:T(8,128)S(1)} %copy-done.1, bf16[2048,128]{1,0:T(8,128)(2,1)S(1)} %bitcast.121, bf16[768,1440]{1,0:T(8,128)(2,1)S(1)} %copy-done), custom_call_target="tpu_custom_call" | custom-call | tf_op jit(solution)/shard_map/pallas_call | solution.py:315
  83.0 0.0 copy-done.10
  83.0 0.2 while.12
  (4 shorter events, 0.0 us)
Async XLA Ops:
  0.6 20.7 %copy-start.2 = (s32[384]{0:T(512)S(1)}, s32[384]{0:T(512)}, u32[]{:S(2)}) copy-start(s32[384]{0:T(512)} %owner_hbm.1) | copy-start | bytes 4612
  5.6 26.2 %copy-start.12 = (s32[8]{0:T(128)S(1)}, s32[8]{0:T(128)}, u32[]{:S(2)}) copy-start(s32[8]{0:T(128)} %param.13) | copy-start | bytes 100
  5.7 43.8 %all-to-all-start.4 = ((bf16[256,2,896]{2,1,0:T(2,128)(2,1)}), bf16[256,2,896]{2,1,0:T(2,128)(2,1)S(1)}, u32[]{:S(2)}, u32[]{:S(2)}) async-start(bf16[256,2,896]{2,1,0:T(2,128)(2,1)} %get-tuple-element.59), calls=%async_computation.4 | async-start | bytes 1835008 | tf_op jit(solution)/shard_map/all_to_all | solution.py:329
  21.3 58.9 %copy-start = (bf16[768,1440]{1,0:T(8,128)(2,1)S(1)}, bf16[768,1440]{1,0:T(8,128)(2,1)}, u32[]{:S(2)}) copy-start(bf16[768,1440]{1,0:T(8,128)(2,1)} %constant.228.clone.waves_ref) | copy-start | bytes 6635524
  21.3 58.8 %copy-start.1 = (f32[8,384]{1,0:T(8,128)S(1)}, f32[8,384]{1,0:T(8,128)}, u32[]{:S(2)}) copy-start(f32[8,384]{1,0:T(8,128)} %get-tuple-element.62.codes_ref) | copy-start | bytes 36868
  53.1 29.9 %copy-start.10 = (bf16[1,8,32,1440]{3,2,1,0:T(8,128)(2,1)S(1)}, bf16[1,8,32,1440]{3,2,1,0:T(8,128)(2,1)}, u32[]{:S(2)}) copy-start(bf16[1,8,32,1440]{3,2,1,0:T(8,128)(2,1)} %param.9) | copy-start | bytes 2211844

commit v4 on v3

--- a/solution.py
+++ b/solution.py
@@ -79,15 +79,11 @@
         table_ref[0:384, 0:384] = rows
         table_ref[0:384, 384:512] = jnp.zeros((384, 128), jnp.bfloat16)
         wide = jnp.concatenate([rows.astype(jnp.float32), jnp.zeros((384, 128), jnp.float32)], axis=1)
-        for shift in range(1, 13):
-            low = max(368 - 32 * shift, 0)
-            high = 400 - 32 * shift
-            if shift == 1:
-                high = 384
-                table_ref[384 + 368:768, :] = wide[368:384].astype(jnp.bfloat16)
-                high = 368
-            moved = pltpu.roll(wide[low:high], 32 * shift, 1)
-            table_ref[384 + low:384 + high, :] = moved.astype(jnp.bfloat16)
+        table_ref[384 + 368:768, :] = wide[368:384].astype(jnp.bfloat16)
+        for step in range(1, 24):
+            low = 368 - 16 * step
+            moved = pltpu.roll(wide[low:low + 16], 16 * step, 1)
+            table_ref[384 + low:384 + low + 16, :] = moved.astype(jnp.bfloat16)
         packed = dot(both, table_ref[...])
         for t in range(4):
             mix_ref[3 + t, pl.ds(r, 256, stride=2), :] = packed[:, 128 * t:128 * t + 128]
@@ -330,7 +326,7 @@
 
 
 def shift_of(order):
-    return jnp.where(order >= 368, 0, (368 - order + 31) // 32 * 32)
+    return jnp.where(order >= 368, 0, (368 - order + 15) // 16 * 16)
 
 
 def ranked(orders):

time: 83.9 us -> 84 us (level)
  no operation moved by 1% of the time
where the time goes in v4:
time: 84 us; the launch traced here: 83.4 us
  blocking collectives  27 us (32%)
  starting transfers between devices  15.7 us (19%)
  waiting for transfers between devices  12.8 us (15%)
  Pallas kernels  11.4 us (14%)
  between operations  6.76 us (8%)
  other arithmetic  5.59 us (7%)
  local copies, waits for them, and re-layouts  3.88 us (5%)
    all_to_all x1, blocking collectives, exchange(): lax.all_to_all(rows, both_axes, split_axis=0, concat_axis=0, tiled=True)  27 us
    all_to_all x1, starting transfers between devices, exchange(): lax.all_to_all(rows, both_axes, split_axis=0, concat_axis=0, tiled=True)  15.7 us
    all_to_all x1, waiting for transfers between devices, exchange(): lax.all_to_all(rows, both_axes, split_axis=0, concat_axis=0, tiled=True)  12.8 us
    pallas_call x1, Pallas kernels, send_call(): pl.pallas_call(send_kernel, out_shape=(jax.ShapeDtypeStruct((256, 2, 896)...  4.99 us
    pallas_call x1, Pallas kernels, score_call(): pl.pallas_call(score_kernel, out_shape=jax.ShapeDtypeStruct((2048, 128),...  3.61 us
    pallas_call x1, Pallas kernels, home_call(): pl.pallas_call(home_kernel, out_shape=(jax.ShapeDtypeStruct((1,), jnp.flo...  2.84 us
    another operation x1, other arithmetic, body(): orders = jnp.stack([full_order, half_order, shift, jnp.max(cutoff)])  1.98 us
    unnamed x11, local copies, waits for them, and re-layouts  1.95 us
  transfers between devices with their start and end apart: 1, of which 1 were waited for; matrix products, arithmetic and copies ran while one was open for 11% of the time, Pallas kernels for 0%

profile of v4, /device:TPU:1, one launch (start us, length us, event | category | flops | bytes accessed | tf_op | source)
XLA Modules:
  0.0 83.4 jit_solution(12382143850474828374)
XLA Ops:
  0.6 0.0 copy-start.2
  0.6 5.0 %shard_map.86 = (bf16[256,2,896]{2,1,0:T(2,128)(2,1)}, f32[8,384]{1,0:T(8,128)}) custom-call(s32[1]{0:T(128)} %bitcast.place_ref, s32[384]{0:T(512)} %owner_hbm.1, bf16[256,1440]{1,0:T(8,128)(2,1)} %bitcast.126, bf16[1440,768]{1,0:T(8,128)(2,1)} %constant.229.clone.waves_hbm, bf16[32,384,384]{2,1,0:T(8,128)(2,1)} %legendre_hbm.1), custom_call_target="tpu_custom_call" | custom-call | tf_op jit(solution)/shard_map/pallas_call | solution.py:124
  5.6 0.0 copy-start.12
  5.7 15.7 %all-to-all-start.4 = ((bf16[256,2,896]{2,1,0:T(2,128)(2,1)}), bf16[256,2,896]{2,1,0:T(2,128)(2,1)S(1)}, u32[]{:S(2)}, u32[]{:S(2)}) async-start(bf16[256,2,896]{2,1,0:T(2,128)(2,1)} %get-tuple-element.59), calls=%async_computation.4 | async-start | bytes 1835008 | tf_op jit(solution)/shard_map/all_to_all | solution.py:325
  21.3 0.0 copy-start
  21.3 0.0 copy-start.1
  21.4 0.0 copy-done.2
  21.4 0.1 dynamic_slice.35
  21.5 0.2 convert_reduce_fusion.1
  21.7 0.8 fusion.63
  25.6 0.1 gt.28
  25.7 0.4 convert_reduce_fusion
  26.1 0.2 select_reduce_fusion
  26.3 0.1 slice.28
  26.4 0.1 slice.47
  27.1 0.1 rev.3
  27.2 0.7 fusion.59
  28.5 1.9 %copy.61 = f32[24,8,2,384]{3,1,2,0:T(8,128)} copy(f32[24,8,2,384]{3,2,1,0:T(2,128)} %param.11) | data formatting | bytes 1179648 | tf_op args[2]
  31.1 0.7 constant_dynamic-slice_fusion
  31.9 0.0 copy-done.12
  31.9 0.6 reduce_max.9
  33.1 0.7 dynamic-slice_bitcast_fusion.2
  33.8 2.0 %pad_add_fusion.1.orders_ref = s32[4]{0:T(128)S(1)} fusion(s32[1]{0:T(128)} %bitcast.6, s32[1]{0:T(128)} %bitcast.5, s32[1]{0:T(128)} %bitcast.4, s32[1]{0:T(128)} %bitcast.3), kind=kLoop, calls=%fused_computation.125 | loop fusion | flops 12 | bytes 32 | tf_op jit(solution)/shard_map/stack | solution.py:422
  35.8 0.7 multiply_reduce_fusion
  36.5 0.1 fusion.52.half_ref
  36.6 12.8 %all-to-all-done.4.got_ref = bf16[256,2,896]{2,1,0:T(2,128)(2,1)S(1)} async-done(((bf16[256,2,896]{2,1,0:T(2,128)(2,1)}), bf16[256,2,896]{2,1,0:T(2,128)(2,1)S(1)}, u32[]{:S(2)}, u32[]{:S(2)}) %all-to-all-start.4) | async-done | bytes 917536 | tf_op jit(solution)/shard_map/all_to_all | solution.py:325
  49.4 0.1 broadcast_in_dim.43.cutoff_ref
  49.5 3.6 %shard_map.87 = bf16[2048,128]{1,0:T(8,128)(2,1)S(1)} custom-call(s32[4]{0:T(128)S(1)} %pad_add_fusion.1.orders_ref, bf16[256,2,896]{2,1,0:T(2,128)(2,1)S(1)} %all-to-all-done.4.got_ref, f32[16,384]{1,0:T(8,128)S(1)} %pad_maximum_fusion.6.full_ref, f32[8,512]{1,0:T(8,128)S(1)} %fusion.52.half_ref, s32[8,128]{1,0:T(8,128)S(1)} %broadcast_in_dim.43.cutoff_ref), custom_call_target="tpu_custom_call" | custom-call | tf_op jit(solution)/shard_map/pallas_call | solution.py:274
  53.1 0.0 copy-start.10
  53.1 27.0 %all_to_all.34 = bf16[256,8,128]{2,1,0:T(8,128)(2,1)S(1)} all-to-all(bf16[256,8,128]{2,1,0:T(8,128)(2,1)S(1)} %bitcast.122), channel_id=1, replica_groups=mesh['ens'=16,'lat'=16] {'lat','ens'}, dimensions={0} | all-to-all | bytes 1048576 | tf_op jit(solution)/shard_map/all_to_all | solution.py:325
  80.1 0.0 copy-done
  80.1 0.0 copy-done.1
  80.1 2.8 %shard_map.88 = (f32[1]{0:T(128)}, bf16[256,1440]{1,0:T(8,128)(2,1)}) custom-call(f32[1]{0:T(128)} %bitcast.2.valid_ref, f32[8,384]{1,0:T(8,128)S(1)} %copy-done.1, bf16[2048,128]{1,0:T(8,128)(2,1)S(1)} %bitcast.121, bf16[768,1440]{1,0:T(8,128)(2,1)S(1)} %copy-done), custom_call_target="tpu_custom_call" | custom-call | tf_op jit(solution)/shard_map/pallas_call | solution.py:311
  83.0 0.0 copy-done.10
  83.0 0.2 while.12
  (4 shorter events, 0.0 us)
Async XLA Ops:
  0.6 20.8 %copy-start.2 = (s32[384]{0:T(512)S(1)}, s32[384]{0:T(512)}, u32[]{:S(2)}) copy-start(s32[384]{0:T(512)} %owner_hbm.1) | copy-start | bytes 4612
  5.6 26.2 %copy-start.12 = (s32[8]{0:T(128)S(1)}, s32[8]{0:T(128)}, u32[]{:S(2)}) copy-start(s32[8]{0:T(128)} %param.13) | copy-start | bytes 100
  5.7 43.8 %all-to-all-start.4 = ((bf16[256,2,896]{2,1,0:T(2,128)(2,1)}), bf16[256,2,896]{2,1,0:T(2,128)(2,1)S(1)}, u32[]{:S(2)}, u32[]{:S(2)}) async-start(bf16[256,2,896]{2,1,0:T(2,128)(2,1)} %get-tuple-element.59), calls=%async_computation.4 | async-start | bytes 1835008 | tf_op jit(solution)/shard_map/all_to_all | solution.py:325
  21.3 58.8 %copy-start = (bf16[768,1440]{1,0:T(8,128)(2,1)S(1)}, bf16[768,1440]{1,0:T(8,128)(2,1)}, u32[]{:S(2)}) copy-start(bf16[768,1440]{1,0:T(8,128)(2,1)} %constant.228.clone.waves_ref) | copy-start | bytes 6635524
  21.3 58.8 %copy-start.1 = (f32[8,384]{1,0:T(8,128)S(1)}, f32[8,384]{1,0:T(8,128)}, u32[]{:S(2)}) copy-start(f32[8,384]{1,0:T(8,128)} %get-tuple-element.62.codes_ref) | copy-start | bytes 36868
  53.1 29.9 %copy-start.10 = (bf16[1,8,32,1440]{3,2,1,0:T(8,128)(2,1)S(1)}, bf16[1,8,32,1440]{3,2,1,0:T(8,128)(2,1)}, u32[]{:S(2)}) copy-start(bf16[1,8,32,1440]{3,2,1,0:T(8,128)(2,1)} %param.9) | copy-start | bytes 2211844

commit v5 on v4

--- a/solution.py
+++ b/solution.py
@@ -54,14 +54,16 @@
     for copy in wave_copies:
         copy.start()
 
+    group = flag(iota((16, 384), 1) // 24 == iota((16, 384), 0))
+    before = flag(iota((384, 384), 0) < iota((384, 384), 1))
+    table_ref[0:384, 384:512] = jnp.zeros((384, 128), jnp.bfloat16)
+    codes_ref[2:8, :] = jnp.zeros((6, 384), jnp.float32)
     owner_copy.wait()
     line = jnp.broadcast_to(owner_ref[...].reshape(1, 384).astype(jnp.float32), (128, 384))
     column = jnp.transpose(line, (1, 0))
     lane = iota((384, 128), 1).astype(jnp.float32)
     held = jnp.concatenate([flag(column == lane + 128.0 * t) for t in range(3)], axis=1)
-    group = flag(iota((16, 384), 1) // 24 == iota((16, 384), 0))
     lat_of = dot(group, held)
-    before = flag(iota((384, 384), 0) < iota((384, 384), 1))
     count = dot(lat_of.astype(jnp.bfloat16), before)
     rank = jnp.sum(lat_of * count, axis=0, keepdims=True)
     lat = jnp.sum(lat_of * iota((16, 384), 0).astype(jnp.float32), axis=0, keepdims=True)
@@ -69,7 +71,6 @@
     half_code = jnp.where(rank >= 16.0, lat * 8.0 + (23.0 - rank), -1.0)
     codes_ref[0:1, :] = full_code
     codes_ref[1:2, :] = half_code
-    codes_ref[2:8, :] = jnp.zeros((6, 384), jnp.float32)
     full, even, odd, half = picks(full_code, half_code)
 
     both = jnp.concatenate([full, half], axis=1)
@@ -77,7 +78,6 @@
     for r in range(2):
         rows = bands_ref[r]
         table_ref[0:384, 0:384] = rows
-        table_ref[0:384, 384:512] = jnp.zeros((384, 128), jnp.bfloat16)
         wide = jnp.concatenate([rows.astype(jnp.float32), jnp.zeros((384, 128), jnp.float32)], axis=1)
         table_ref[384 + 368:768, :] = wide[368:384].astype(jnp.bfloat16)
         for step in range(1, 24):
@@ -197,11 +197,10 @@
     total_ref[...] = jnp.zeros((8, 128), jnp.float32)
     full_order, half_order, shift, highest = [orders_ref[i] for i in range(4)]
 
-    @pl.loop(0, 6)
-    def _(step):
+    def full_step(step):
         part = step // 3
         third = step % 3
-        lanes = pl.ds(pl.multiple_of(third * 128, 128), 128)
+        lanes = pl.ds(third * 128, 128)
         first = third * 128
         active = (first + 127 >= full_order) & (first <= highest)
 
@@ -209,16 +208,19 @@
             return coeffs_ref[third, pl.ds(2 * e + part, 8, stride=32), :]
 
         def store(e, value):
-            grads_ref[pl.ds(pl.multiple_of(part * 128 + 8 * e, 8), 8), lanes] = value
+            grads_ref[pl.ds(part * 128 + 8 * e, 8), lanes] = value
 
         @pl.when(active)
         def _():
-            goal = full_ref[pl.ds(pl.multiple_of(part * 8, 8), 8), lanes]
+            goal = full_ref[pl.ds(part * 8, 8), lanes]
             column(iota((8, 128), 1) + first, full_order, goal, load, store)
 
         @pl.when(jnp.logical_not(active))
         def _():
-            grads_ref[pl.ds(pl.multiple_of(part * 128, 128), 128), lanes] = jnp.zeros((128, 128), jnp.float32)
+            grads_ref[pl.ds(part * 128, 128), lanes] = jnp.zeros((128, 128), jnp.float32)
+
+    for step in range(6):
+        full_step(step)
 
     @pl.loop(0, 4)
     def _(tile):

time: 84 us -> 83.8 us (level)
  no operation moved by 1% of the time
where the time goes in v5:
time: 83.8 us; the launch traced here: 83.1 us
  blocking collectives  26.8 us (32%)
  starting transfers between devices  15.7 us (19%)
  waiting for transfers between devices  12.8 us (15%)
  Pallas kernels  11.3 us (13%)
  between operations  6.76 us (8%)
  other arithmetic  5.59 us (7%)
  local copies, waits for them, and re-layouts  3.88 us (5%)
    all_to_all x1, blocking collectives, exchange(): lax.all_to_all(rows, both_axes, split_axis=0, concat_axis=0, tiled=True)  26.8 us
    all_to_all x1, starting transfers between devices, exchange(): lax.all_to_all(rows, both_axes, split_axis=0, concat_axis=0, tiled=True)  15.7 us
    all_to_all x1, waiting for transfers between devices, exchange(): lax.all_to_all(rows, both_axes, split_axis=0, concat_axis=0, tiled=True)  12.8 us
    pallas_call x1, Pallas kernels, send_call(): pl.pallas_call(send_kernel, out_shape=(jax.ShapeDtypeStruct((256, 2, 896)...  4.97 us
    pallas_call x1, Pallas kernels, score_call(): pl.pallas_call(score_kernel, out_shape=jax.ShapeDtypeStruct((2048, 128),...  3.5 us
    pallas_call x1, Pallas kernels, home_call(): pl.pallas_call(home_kernel, out_shape=(jax.ShapeDtypeStruct((1,), jnp.flo...  2.84 us
    another operation x1, other arithmetic, body(): orders = jnp.stack([full_order, half_order, shift, jnp.max(cutoff)])  1.98 us
    unnamed x11, local copies, waits for them, and re-layouts  1.95 us
  transfers between devices with their start and end apart: 1, of which 1 were waited for; matrix products, arithmetic and copies ran while one was open for 11% of the time, Pallas kernels for 0%

profile of v5, /device:TPU:1, one launch (start us, length us, event | category | flops | bytes accessed | tf_op | source)
XLA Modules:
  0.0 83.1 jit_solution(4343460821531890359)
XLA Ops:
  0.6 0.0 copy-start.2
  0.6 5.0 %shard_map.86 = (bf16[256,2,896]{2,1,0:T(2,128)(2,1)}, f32[8,384]{1,0:T(8,128)}) custom-call(s32[1]{0:T(128)} %bitcast.place_ref, s32[384]{0:T(512)} %owner_hbm.1, bf16[256,1440]{1,0:T(8,128)(2,1)} %bitcast.126, bf16[1440,768]{1,0:T(8,128)(2,1)} %constant.229.clone.waves_hbm, bf16[32,384,384]{2,1,0:T(8,128)(2,1)} %legendre_hbm.1), custom_call_target="tpu_custom_call" | custom-call | tf_op jit(solution)/shard_map/pallas_call | solution.py:124
  5.6 0.0 copy-start.12
  5.6 15.7 %all-to-all-start.4 = ((bf16[256,2,896]{2,1,0:T(2,128)(2,1)}), bf16[256,2,896]{2,1,0:T(2,128)(2,1)S(1)}, u32[]{:S(2)}, u32[]{:S(2)}) async-start(bf16[256,2,896]{2,1,0:T(2,128)(2,1)} %get-tuple-element.59), calls=%async_computation.4 | async-start | bytes 1835008 | tf_op jit(solution)/shard_map/all_to_all | solution.py:327
  21.3 0.0 copy-start
  21.3 0.0 copy-start.1
  21.4 0.0 copy-done.2
  21.4 0.1 dynamic_slice.35
  21.5 0.2 convert_reduce_fusion.1
  21.6 0.8 fusion.63
  25.6 0.1 gt.28
  25.7 0.4 convert_reduce_fusion
  26.1 0.2 select_reduce_fusion
  26.3 0.1 slice.28
  26.4 0.1 slice.47
  27.1 0.1 rev.3
  27.2 0.7 fusion.59
  28.5 1.9 %copy.61 = f32[24,8,2,384]{3,1,2,0:T(8,128)} copy(f32[24,8,2,384]{3,2,1,0:T(2,128)} %param.11) | data formatting | bytes 1179648 | tf_op args[2]
  31.1 0.7 constant_dynamic-slice_fusion
  31.8 0.0 copy-done.12
  31.9 0.6 reduce_max.9
  33.1 0.7 dynamic-slice_bitcast_fusion.2
  33.8 2.0 %pad_add_fusion.1.orders_ref = s32[4]{0:T(128)S(1)} fusion(s32[1]{0:T(128)} %bitcast.6, s32[1]{0:T(128)} %bitcast.5, s32[1]{0:T(128)} %bitcast.4, s32[1]{0:T(128)} %bitcast.3), kind=kLoop, calls=%fused_computation.125 | loop fusion | flops 12 | bytes 32 | tf_op jit(solution)/shard_map/stack | solution.py:424
  35.8 0.7 multiply_reduce_fusion
  36.5 0.1 fusion.52.half_ref
  36.6 12.8 %all-to-all-done.4.got_ref = bf16[256,2,896]{2,1,0:T(2,128)(2,1)S(1)} async-done(((bf16[256,2,896]{2,1,0:T(2,128)(2,1)}), bf16[256,2,896]{2,1,0:T(2,128)(2,1)S(1)}, u32[]{:S(2)}, u32[]{:S(2)}) %all-to-all-start.4) | async-done | bytes 917536 | tf_op jit(solution)/shard_map/all_to_all | solution.py:327
  49.4 0.1 broadcast_in_dim.43.cutoff_ref
  49.5 3.5 %shard_map.87 = bf16[2048,128]{1,0:T(8,128)(2,1)S(1)} custom-call(s32[4]{0:T(128)S(1)} %pad_add_fusion.1.orders_ref, bf16[256,2,896]{2,1,0:T(2,128)(2,1)S(1)} %all-to-all-done.4.got_ref, f32[16,384]{1,0:T(8,128)S(1)} %pad_maximum_fusion.6.full_ref, f32[8,512]{1,0:T(8,128)S(1)} %fusion.52.half_ref, s32[8,128]{1,0:T(8,128)S(1)} %broadcast_in_dim.43.cutoff_ref), custom_call_target="tpu_custom_call" | custom-call | tf_op jit(solution)/shard_map/pallas_call | solution.py:276
  53.0 0.0 copy-start.10
  53.0 26.8 %all_to_all.34 = bf16[256,8,128]{2,1,0:T(8,128)(2,1)S(1)} all-to-all(bf16[256,8,128]{2,1,0:T(8,128)(2,1)S(1)} %bitcast.122), channel_id=1, replica_groups=mesh['ens'=16,'lat'=16] {'lat','ens'}, dimensions={0} | all-to-all | bytes 1048576 | tf_op jit(solution)/shard_map/all_to_all | solution.py:327
  79.8 0.0 copy-done
  79.8 0.0 copy-done.1
  79.8 2.8 %shard_map.88 = (f32[1]{0:T(128)}, bf16[256,1440]{1,0:T(8,128)(2,1)}) custom-call(f32[1]{0:T(128)} %bitcast.2.valid_ref, f32[8,384]{1,0:T(8,128)S(1)} %copy-done.1, bf16[2048,128]{1,0:T(8,128)(2,1)S(1)} %bitcast.121, bf16[768,1440]{1,0:T(8,128)(2,1)S(1)} %copy-done), custom_call_target="tpu_custom_call" | custom-call | tf_op jit(solution)/shard_map/pallas_call | solution.py:313
  82.7 0.0 copy-done.10
  82.7 0.2 while.12
  (4 shorter events, 0.0 us)
Async XLA Ops:
  0.6 20.7 %copy-start.2 = (s32[384]{0:T(512)S(1)}, s32[384]{0:T(512)}, u32[]{:S(2)}) copy-start(s32[384]{0:T(512)} %owner_hbm.1) | copy-start | bytes 4612
  5.6 26.2 %copy-start.12 = (s32[8]{0:T(128)S(1)}, s32[8]{0:T(128)}, u32[]{:S(2)}) copy-start(s32[8]{0:T(128)} %param.13) | copy-start | bytes 100
  5.6 43.8 %all-to-all-start.4 = ((bf16[256,2,896]{2,1,0:T(2,128)(2,1)}), bf16[256,2,896]{2,1,0:T(2,128)(2,1)S(1)}, u32[]{:S(2)}, u32[]{:S(2)}) async-start(bf16[256,2,896]{2,1,0:T(2,128)(2,1)} %get-tuple-element.59), calls=%async_computation.4 | async-start | bytes 1835008 | tf_op jit(solution)/shard_map/all_to_all | solution.py:327
  21.3 58.5 %copy-start = (bf16[768,1440]{1,0:T(8,128)(2,1)S(1)}, bf16[768,1440]{1,0:T(8,128)(2,1)}, u32[]{:S(2)}) copy-start(bf16[768,1440]{1,0:T(8,128)(2,1)} %constant.228.clone.waves_ref) | copy-start | bytes 6635524
  21.3 58.5 %copy-start.1 = (f32[8,384]{1,0:T(8,128)S(1)}, f32[8,384]{1,0:T(8,128)}, u32[]{:S(2)}) copy-start(f32[8,384]{1,0:T(8,128)} %get-tuple-element.62.codes_ref) | copy-start | bytes 36868
  53.0 29.7 %copy-start.10 = (bf16[1,8,32,1440]{3,2,1,0:T(8,128)(2,1)S(1)}, bf16[1,8,32,1440]{3,2,1,0:T(8,128)(2,1)}, u32[]{:S(2)}) copy-start(bf16[1,8,32,1440]{3,2,1,0:T(8,128)(2,1)} %param.9) | copy-start | bytes 2211844

commit v6 on v5

--- a/solution.py
+++ b/solution.py
@@ -174,14 +174,16 @@
         member = [load(e) for e in range(16)]
         slope = [jnp.zeros((8, 128), jnp.float32) for _ in range(16)]
         rest = jnp.zeros((8, 128), jnp.float32)
-        for i in range(16):
+        for i in range(15):
+            group = jnp.full((8, 128), (i - 15.0) / delta_abs, jnp.float32)
             for k in range(i + 1, 16):
                 spread = member[i] - member[k]
                 inverse = lax.rsqrt(spread * spread + offset)
                 step_slope = spread * inverse
                 slope[i] = slope[i] + step_slope
                 slope[k] = slope[k] - step_slope
-                rest = rest + (inverse - 1.0 / delta_abs)
+                group = group + inverse
+            rest = rest + group
         pair_value = offset * rest
         for i in range(1, 16):
             pair_value = pair_value + (member[i] - member[0]) * slope[i]

time: 83.8 us -> 83.7 us (level)
  no operation moved by 1% of the time
where the time goes in v6:
time: 83.7 us; the launch traced here: 83.4 us
  blocking collectives  27.2 us (32%)
  starting transfers between devices  15.7 us (19%)
  waiting for transfers between devices  12.8 us (15%)
  Pallas kernels  11.2 us (13%)
  between operations  6.76 us (8%)
  other arithmetic  5.59 us (7%)
  local copies, waits for them, and re-layouts  3.88 us (5%)
    all_to_all x1, blocking collectives, exchange(): lax.all_to_all(rows, both_axes, split_axis=0, concat_axis=0, tiled=True)  27.2 us
    all_to_all x1, starting transfers between devices, exchange(): lax.all_to_all(rows, both_axes, split_axis=0, concat_axis=0, tiled=True)  15.7 us
    all_to_all x1, waiting for transfers between devices, exchange(): lax.all_to_all(rows, both_axes, split_axis=0, concat_axis=0, tiled=True)  12.8 us
    pallas_call x1, Pallas kernels, send_call(): pl.pallas_call(send_kernel, out_shape=(jax.ShapeDtypeStruct((256, 2, 896)...  4.97 us
    pallas_call x1, Pallas kernels, score_call(): pl.pallas_call(score_kernel, out_shape=jax.ShapeDtypeStruct((2048, 128),...  3.38 us
    pallas_call x1, Pallas kernels, home_call(): pl.pallas_call(home_kernel, out_shape=(jax.ShapeDtypeStruct((1,), jnp.flo...  2.84 us
    another operation x1, other arithmetic, body(): orders = jnp.stack([full_order, half_order, shift, jnp.max(cutoff)])  1.98 us
    unnamed x11, local copies, waits for them, and re-layouts  1.95 us
  transfers between devices with their start and end apart: 1, of which 1 were waited for; matrix products, arithmetic and copies ran while one was open for 11% of the time, Pallas kernels for 0%

profile of v6, /device:TPU:1, one launch (start us, length us, event | category | flops | bytes accessed | tf_op | source)
XLA Modules:
  0.0 83.4 jit_solution(13524403904875048522)
XLA Ops:
  0.6 0.0 copy-start.2
  0.6 5.0 %shard_map.86 = (bf16[256,2,896]{2,1,0:T(2,128)(2,1)}, f32[8,384]{1,0:T(8,128)}) custom-call(s32[1]{0:T(128)} %bitcast.place_ref, s32[384]{0:T(512)} %owner_hbm.1, bf16[256,1440]{1,0:T(8,128)(2,1)} %bitcast.126, bf16[1440,768]{1,0:T(8,128)(2,1)} %constant.229.clone.waves_hbm, bf16[32,384,384]{2,1,0:T(8,128)(2,1)} %legendre_hbm.1), custom_call_target="tpu_custom_call" | custom-call | tf_op jit(solution)/shard_map/pallas_call | solution.py:124
  5.6 0.0 copy-start.12
  5.6 15.7 %all-to-all-start.4 = ((bf16[256,2,896]{2,1,0:T(2,128)(2,1)}), bf16[256,2,896]{2,1,0:T(2,128)(2,1)S(1)}, u32[]{:S(2)}, u32[]{:S(2)}) async-start(bf16[256,2,896]{2,1,0:T(2,128)(2,1)} %get-tuple-element.59), calls=%async_computation.4 | async-start | bytes 1835008 | tf_op jit(solution)/shard_map/all_to_all | solution.py:329
  21.3 0.0 copy-start
  21.3 0.0 copy-start.1
  21.4 0.0 copy-done.2
  21.4 0.1 dynamic_slice.35
  21.5 0.2 convert_reduce_fusion.1
  21.6 0.8 fusion.63
  25.6 0.1 gt.28
  25.7 0.4 convert_reduce_fusion
  26.1 0.2 select_reduce_fusion
  26.3 0.1 slice.28
  26.4 0.1 slice.47
  27.1 0.1 rev.3
  27.2 0.7 fusion.59
  28.5 1.9 %copy.61 = f32[24,8,2,384]{3,1,2,0:T(8,128)} copy(f32[24,8,2,384]{3,2,1,0:T(2,128)} %param.11) | data formatting | bytes 1179648 | tf_op args[2]
  31.1 0.7 constant_dynamic-slice_fusion
  31.8 0.0 copy-done.12
  31.9 0.6 reduce_max.9
  33.1 0.7 dynamic-slice_bitcast_fusion.2
  33.8 2.0 %pad_add_fusion.1.orders_ref = s32[4]{0:T(128)S(1)} fusion(s32[1]{0:T(128)} %bitcast.6, s32[1]{0:T(128)} %bitcast.5, s32[1]{0:T(128)} %bitcast.4, s32[1]{0:T(128)} %bitcast.3), kind=kLoop, calls=%fused_computation.125 | loop fusion | flops 12 | bytes 32 | tf_op jit(solution)/shard_map/stack | solution.py:426
  35.8 0.7 multiply_reduce_fusion
  36.5 0.1 fusion.52.half_ref
  36.6 12.8 %all-to-all-done.4.got_ref = bf16[256,2,896]{2,1,0:T(2,128)(2,1)S(1)} async-done(((bf16[256,2,896]{2,1,0:T(2,128)(2,1)}), bf16[256,2,896]{2,1,0:T(2,128)(2,1)S(1)}, u32[]{:S(2)}, u32[]{:S(2)}) %all-to-all-start.4) | async-done | bytes 917536 | tf_op jit(solution)/shard_map/all_to_all | solution.py:329
  49.4 0.1 broadcast_in_dim.43.cutoff_ref
  49.5 3.4 %shard_map.87 = bf16[2048,128]{1,0:T(8,128)(2,1)S(1)} custom-call(s32[4]{0:T(128)S(1)} %pad_add_fusion.1.orders_ref, bf16[256,2,896]{2,1,0:T(2,128)(2,1)S(1)} %all-to-all-done.4.got_ref, f32[16,384]{1,0:T(8,128)S(1)} %pad_maximum_fusion.6.full_ref, f32[8,512]{1,0:T(8,128)S(1)} %fusion.52.half_ref, s32[8,128]{1,0:T(8,128)S(1)} %broadcast_in_dim.43.cutoff_ref), custom_call_target="tpu_custom_call" | custom-call | tf_op jit(solution)/shard_map/pallas_call | solution.py:278
  52.9 0.0 copy-start.10
  52.9 27.2 %all_to_all.34 = bf16[256,8,128]{2,1,0:T(8,128)(2,1)S(1)} all-to-all(bf16[256,8,128]{2,1,0:T(8,128)(2,1)S(1)} %bitcast.122), channel_id=1, replica_groups=mesh['ens'=16,'lat'=16] {'lat','ens'}, dimensions={0} | all-to-all | bytes 1048576 | tf_op jit(solution)/shard_map/all_to_all | solution.py:329
  80.1 0.0 copy-done
  80.1 0.0 copy-done.1
  80.1 2.8 %shard_map.88 = (f32[1]{0:T(128)}, bf16[256,1440]{1,0:T(8,128)(2,1)}) custom-call(f32[1]{0:T(128)} %bitcast.2.valid_ref, f32[8,384]{1,0:T(8,128)S(1)} %copy-done.1, bf16[2048,128]{1,0:T(8,128)(2,1)S(1)} %bitcast.121, bf16[768,1440]{1,0:T(8,128)(2,1)S(1)} %copy-done), custom_call_target="tpu_custom_call" | custom-call | tf_op jit(solution)/shard_map/pallas_call | solution.py:315
  83.0 0.0 copy-done.10
  83.0 0.2 while.12
  (4 shorter events, 0.0 us)
Async XLA Ops:
  0.6 20.7 %copy-start.2 = (s32[384]{0:T(512)S(1)}, s32[384]{0:T(512)}, u32[]{:S(2)}) copy-start(s32[384]{0:T(512)} %owner_hbm.1) | copy-start | bytes 4612
  5.6 26.2 %copy-start.12 = (s32[8]{0:T(128)S(1)}, s32[8]{0:T(128)}, u32[]{:S(2)}) copy-start(s32[8]{0:T(128)} %param.13) | copy-start | bytes 100
  5.6 43.8 %all-to-all-start.4 = ((bf16[256,2,896]{2,1,0:T(2,128)(2,1)}), bf16[256,2,896]{2,1,0:T(2,128)(2,1)S(1)}, u32[]{:S(2)}, u32[]{:S(2)}) async-start(bf16[256,2,896]{2,1,0:T(2,128)(2,1)} %get-tuple-element.59), calls=%async_computation.4 | async-start | bytes 1835008 | tf_op jit(solution)/shard_map/all_to_all | solution.py:329
  21.3 58.8 %copy-start = (bf16[768,1440]{1,0:T(8,128)(2,1)S(1)}, bf16[768,1440]{1,0:T(8,128)(2,1)}, u32[]{:S(2)}) copy-start(bf16[768,1440]{1,0:T(8,128)(2,1)} %constant.228.clone.waves_ref) | copy-start | bytes 6635524
  21.3 58.8 %copy-start.1 = (f32[8,384]{1,0:T(8,128)S(1)}, f32[8,384]{1,0:T(8,128)}, u32[]{:S(2)}) copy-start(f32[8,384]{1,0:T(8,128)} %get-tuple-element.62.codes_ref) | copy-start | bytes 36868
  52.9 30.1 %copy-start.10 = (bf16[1,8,32,1440]{3,2,1,0:T(8,128)(2,1)S(1)}, bf16[1,8,32,1440]{3,2,1,0:T(8,128)(2,1)}, u32[]{:S(2)}) copy-start(bf16[1,8,32,1440]{3,2,1,0:T(8,128)(2,1)} %param.9) | copy-start | bytes 2211844
